TPU v7x, 32 devices: a whole 2x2x4 slice. The times are simulated.
32 devices in a mesh: seq: 8 (over y, x, core), tp: 4 (over z).
Axes of the slice: x: 2, y: 2, z: 4, core: 2. Of those that a mesh axis runs over, the one named last changes fastest.
Arguments:
- embeddings: bfloat16 [3072, 4096], P('seq', 'tp'), may hold values from -6 to 6
- span_mask: int32 [3072], P('seq'), may hold values from 0 to 1, as said below
- sentinel_id: int32 [3072], P('seq'), may hold values from 0 to 99, as said below
- sentinel_table: bfloat16 [100, 4096], P(None, 'tp'), may hold values from -6 to 6
- gen_weight: bfloat16 [4096, 240], P(None, 'tp'), may hold values from -0.1875 to 0.1875
- up_weight: bfloat16 [4096, 8192], P(None, 'tp'), may hold values from -0.09375 to 0.09375
- down_weight: bfloat16 [8192, 4096], P('tp'), may hold values from -0.0625 to 0.0625
- cotangent: bfloat16 [3072, 4096], P('seq', 'tp'), may hold values from -0.59765625 to 0.59765625
Outputs:
- layer_output: bfloat16 [3072, 4096], P('seq', 'tp')
- embed_grad: float32 [3072, 4096], P('seq', 'tp')
- table_grad: float32 [100, 4096], P(None, 'tp')
- gen_grad: float32 [4096, 240], P(None, 'tp')
- up_grad: float32 [4096, 8192], P('seq', 'tp')
- down_grad: float32 [8192, 4096], P('tp', 'seq')
Inputs may be any that keep to these rules, and one draw needn't show every extreme that they name: `span_mask`: the tokens fall into aligned blocks of 16; each block holds exactly one span of 1 to 3 consecutive tokens marked 1, the rest 0. `sentinel_id`: all 16 tokens of an aligned block carry the same sentinel id.
All inputs are finite; a program needn't handle non-finite values.
Results may differ from a plain program's by a relative error of at most 0.035.
Values may be sent and summed in bfloat16 or wider, within the bound.
A program may use at most 192 MiB of HBM per device.

v0:
```python
import jax
import jax.numpy as jnp
from jax import lax
from jax.sharding import PartitionSpec as P

KW = 15
SENT = 100


def with_halo(block, sides, width):
    for axis, dim in sides:
        count = lax.axis_size(axis)
        forward = [(i, i + 1) for i in range(count - 1)]
        backward = [(target, source) for source, target in forward]
        low = lax.ppermute(
            lax.slice_in_dim(block, block.shape[dim] - width, None, axis=dim), axis, forward
        )
        high = lax.ppermute(lax.slice_in_dim(block, 0, width, axis=dim), axis, backward)
        block = jnp.concatenate([low, block, high], axis=dim)
    return block


def gelu_tanh(values):
    return jax.nn.gelu(values, approximate=True)


def body(
    embeddings,
    span_mask,
    sentinel_id,
    sentinel_table,
    gen_weight,
    up_weight,
    down_weight,
    cotangent,
):
    tok_rows, feat_width = embeddings.shape
    head_count = gen_weight.shape[1] // KW
    head_width = feat_width // head_count
    tap_reach = (KW - 1) // 2
    sentinel_codes = jnp.arange(SENT, dtype=jnp.int32)
    onehot = sentinel_id[:, None] == sentinel_codes[None, :]
    picked = jnp.dot(
        onehot.astype(jnp.bfloat16), sentinel_table, preferred_element_type=jnp.float32
    ).astype(jnp.bfloat16)
    masked = span_mask[:, None] == 1
    hidden = jnp.where(masked, picked, embeddings)
    full_hidden = lax.all_gather(hidden, "tp", axis=1, tiled=True)
    logits = jnp.dot(full_hidden, gen_weight, preferred_element_type=jnp.float32)
    exp_logits = jnp.exp(logits.reshape(tok_rows, head_count, KW))
    kernel = exp_logits / jnp.sum(exp_logits, axis=-1, keepdims=True)
    padded = with_halo(hidden, (("seq", 0),), tap_reach)
    padded = padded.reshape(tok_rows + 2 * tap_reach, head_count, head_width)
    conv_sum = jnp.zeros((tok_rows, head_count, head_width), jnp.float32)
    for tap_index in range(KW):
        conv_sum = (
            conv_sum + kernel[:, :, tap_index, None] * padded[tap_index : tap_index + tok_rows]
        )
    act = (hidden.astype(jnp.float32) + conv_sum.reshape(tok_rows, feat_width)).astype(jnp.bfloat16)
    shard_piece = lax.all_gather(act, "tp", axis=1, tiled=True)
    up_rows = up_weight
    pre_sum = jnp.dot(shard_piece, up_rows, preferred_element_type=jnp.float32)
    full_copy = shard_piece
    middle, gelu_back = jax.vjp(gelu_tanh, pre_sum)
    middle = middle.astype(jnp.bfloat16)
    down_cols = down_weight
    ffn_total = lax.psum_scatter(
        lax.dot_general(
            down_cols, middle, (((0,), (1,)), ((), ())), preferred_element_type=jnp.float32
        ).astype(jnp.bfloat16),
        "tp",
        scatter_dimension=0,
        tiled=True,
    ).astype(jnp.float32)
    layer_output = (act.astype(jnp.float32) + ffn_total.T).astype(jnp.bfloat16)
    shard_piece = lax.all_gather(cotangent, "tp", axis=1, tiled=True)
    down_cols = down_weight
    middle_sum = lax.dot_general(
        shard_piece, down_cols, (((1,), (1,)), ((), ())), preferred_element_type=jnp.float32
    )
    block_term = lax.dot_general(
        middle, shard_piece, (((0,), (0,)), ((), ())), preferred_element_type=jnp.float32
    )
    down_term = block_term
    middle_grad, down_term = (middle_sum, down_term)
    down_grad = lax.psum_scatter(
        down_term.astype(jnp.bfloat16), "seq", scatter_dimension=1, tiled=True
    ).astype(jnp.float32)
    pre_grad = gelu_back(middle_grad)[0].astype(jnp.bfloat16)
    up_grad = lax.psum_scatter(
        lax.dot_general(
            full_copy, pre_grad, (((0,), (0,)), ((), ())), preferred_element_type=jnp.float32
        ).astype(jnp.bfloat16),
        "seq",
        scatter_dimension=0,
        tiled=True,
    ).astype(jnp.float32)
    up_rows = up_weight
    act_back = lax.psum_scatter(
        lax.dot_general(
            up_rows, pre_grad, (((1,), (1,)), ((), ())), preferred_element_type=jnp.float32
        ).astype(jnp.bfloat16),
        "tp",
        scatter_dimension=0,
        tiled=True,
    ).astype(jnp.float32)
    act_grad = cotangent.astype(jnp.float32) + act_back.T
    act_three = act_grad.reshape(tok_rows, head_count, head_width)
    kernel_grad = jnp.stack(
        [
            jnp.sum(act_three * padded[tap_index : tap_index + tok_rows], axis=-1)
            for tap_index in range(KW)
        ],
        axis=-1,
    )
    weighted = jnp.sum(kernel * kernel_grad, axis=-1, keepdims=True)
    logit_grad = (
        (kernel * (kernel_grad - weighted)).reshape(tok_rows, head_count * KW).astype(jnp.bfloat16)
    )
    joined = jnp.concatenate([act_grad, kernel.reshape(tok_rows, head_count * KW)], axis=1)
    joined_pad = with_halo(joined.astype(jnp.bfloat16), (("seq", 0),), tap_reach).astype(
        joined.dtype
    )
    grad_pad = joined_pad[:, :feat_width].reshape(tok_rows + 2 * tap_reach, head_count, head_width)
    kernel_pad = joined_pad[:, feat_width:].reshape(tok_rows + 2 * tap_reach, head_count, KW)
    conv_back = jnp.zeros((tok_rows, head_count, head_width), jnp.float32)
    for tap_index in range(KW):
        lower = 2 * tap_reach - tap_index
        conv_back = (
            conv_back
            + kernel_pad[lower : lower + tok_rows, :, tap_index, None]
            * grad_pad[lower : lower + tok_rows]
        )
    gen_part = lax.dot_general(
        full_hidden, logit_grad, (((0,), (0,)), ((), ())), preferred_element_type=jnp.float32
    )
    gen_back = (
        lax.psum_scatter(
            lax.dot_general(
                gen_weight, logit_grad, (((1,), (1,)), ((), ())), preferred_element_type=jnp.float32
            ).astype(jnp.bfloat16),
            "tp",
            scatter_dimension=0,
            tiled=True,
        )
        .astype(jnp.float32)
        .T
    )
    hidden_grad = act_grad + conv_back.reshape(tok_rows, feat_width) + gen_back
    embed_grad = jnp.where(masked, jnp.float32(0.0), hidden_grad)
    table_part = jnp.dot(
        onehot.astype(jnp.float32).T,
        jnp.where(masked, hidden_grad, jnp.float32(0.0)),
        precision=lax.Precision.HIGHEST,
    )
    gen_sum, table_grad = (
        lax.psum(gen_part.astype(jnp.bfloat16), "seq").astype(jnp.float32),
        lax.psum(table_part.astype(jnp.bfloat16), "seq").astype(jnp.float32),
    )
    return (layer_output, embed_grad, table_grad, gen_sum, up_grad, down_grad)


def solution(mesh):
    placed = (
        P("seq", "tp"),
        P("seq"),
        P("seq"),
        P(None, "tp"),
        P(None, "tp"),
        P(None, "tp"),
        P("tp", None),
        P("seq", "tp"),
    )
    return jax.shard_map(
        body,
        mesh=mesh,
        in_specs=placed,
        out_specs=(
            P("seq", "tp"),
            P("seq", "tp"),
            P(None, "tp"),
            P(None, "tp"),
            P("seq", "tp"),
            P("tp", "seq"),
        ),
        check_vma=False,
    )
```

profile of v0, /device:TPU:0, one launch (start us, length us, event | category | flops | bytes accessed | tf_op | source)
XLA Modules:
  0.0 792.7 jit_solution(6829392580984858759)
XLA Ops:
  8.0 2.6 fusion.45
  12.3 2.3 collective-permute-start
  15.9 60.9 %all-gather.4.cloned.1.call-done = bf16[384,4096]{1,0:T(8,128)(2,1)} async-done(((bf16[384,1024]{1,0:T(8,128)(2,1)}), bf16[384,4096]{1,0:T(8,128)(2,1)}) %all-gather.4.cloned.1.call-update) | async-done | bytes 3145744 | tf_op jit(solution)/shard_map/all_gather | solution.py:48
  76.9 3.0 convolution_exponential_fusion
  98.8 1.5 copy.263
  108.4 7.3 fusion.44
  115.8 25.0 %all-gather.8.cloned.1.call-done = bf16[384,4096]{1,0:T(8,128)(2,1)} async-done(((bf16[384,1024]{1,0:T(8,128)(2,1)}), bf16[384,4096]{1,0:T(8,128)(2,1)}) %all-gather.8.cloned.1.call-update) | async-done | bytes 3145744 | tf_op jit(solution)/shard_map/all_gather | solution.py:76
  140.7 12.3 %fusion.73 = f32[384,2048]{1,0:T(8,128)} fusion(bf16[384,4096]{1,0:T(8,128)(2,1)} %all-gather.8.cloned.1.call-done, bf16[2048,4096]{1,0:T(8,128)(2,1)} %param.14), kind=kOutput, calls=%fused_computation.153 | convolution fusion | flops 6442450944 | bytes 23068672 | tf_op jit(solution)/shard_map/dot_general | solution.py:78
  153.0 52.0 %all-gather.6.cloned.1.call-done = bf16[384,4096]{1,0:T(8,128)(2,1)} async-done(((bf16[384,1024]{1,0:T(8,128)(2,1)}), bf16[384,4096]{1,0:T(8,128)(2,1)}) %all-gather.6.cloned.1.call-update) | async-done | bytes 3145744 | tf_op jit(solution)/shard_map/all_gather | solution.py:60
  205.0 14.3 %fusion.10 = (bf16[384,2048]{1,0:T(8,128)(2,1)S(1)}, f32[384,2048]{1,0:T(8,128)}) fusion(f32[384,2048]{1,0:T(8,128)} %fusion.73, bf16[384,4096]{1,0:T(8,128)(2,1)} %all-gather.6.cloned.1.call-done, bf16[4096,2048]{1,0:T(8,128)(2,1)} %param.13), kind=kOutput, calls=%fused_computation.18 | convolution fusion | flops 6458179584 | bytes 27787264 | tf_op jit(solution)/shard_map/dot_general | solution.py:62
  220.5 11.4 %fusion.2 = bf16[4096,384]{0,1:T(8,128)(2,1)} fusion(bf16[384,2048]{1,0:T(8,128)(2,1)S(1)} %get-tuple-element.62, bf16[4096,2048]{1,0:T(8,128)(2,1)} %param.13), kind=kOutput, calls=%fused_computation.7 | convolution fusion | flops 6444023808 | bytes 21495808 | tf_op jit(solution)/shard_map/dot_general | solution.py:100
  232.2 58.8 %reduce-scatter.8.cloned.1.call-done = bf16[1024,384]{0,1:T(8,128)(2,1)} async-done(((bf16[4096,384]{0,1:T(8,128)(2,1)}), bf16[1024,384]{0,1:T(8,128)(2,1)}) %reduce-scatter.8.cloned.1.call-update) | async-done | bytes 786448 | tf_op jit(solution)/shard_map/reduce_scatter | solution.py:99
  291.0 5.6 convert_multiply_fusion.16
  296.6 2.9 mul.679
  299.5 1.9 reduce_sum.160
  301.5 2.9 mul.667
  304.3 1.9 reduce_sum.154
  306.3 2.9 mul.669
  309.2 1.9 reduce_sum.155
  311.2 2.9 mul.671
  314.1 1.9 reduce_sum.156
  316.1 2.9 mul.673
  318.9 1.9 reduce_sum.157
  320.9 2.9 mul.675
  323.8 1.9 reduce_sum.158
  325.8 2.9 mul.677
  328.7 2.0 reduce_sum.159
  330.7 5.1 convert_multiply_fusion.2
  335.8 2.0 mul.695
  338.4 2.4 mul.683
  341.3 2.0 mul.685
  343.9 2.0 mul.687
  346.5 2.0 mul.689
  349.1 2.0 mul.691
  351.7 2.0 mul.693
  354.3 2.0 mul.681
  357.4 2.7 fusion.3
  360.2 14.7 %fusion.1 = bf16[4096,384]{0,1:T(8,128)(2,1)} fusion(bf16[2048,4096]{1,0:T(8,128)(2,1)} %param.14, f32[384,2048]{1,0:T(8,128)} %get-tuple-element.63), kind=kOutput, calls=%fused_computation.6 | convolution fusion | flops 6451101696 | bytes 23068672 | tf_op jit(solution)/shard_map/dot_general | solution.py:68
  377.6 1.6 collective-permute-start.3
  379.2 3.3 convolution_convert_fusion.5
  385.0 1.5 copy.218
  386.5 1.5 copy.217
  388.0 1.5 copy.216
  399.5 1.5 copy.269
  403.5 1.5 copy.271
  407.5 1.5 copy.273
  413.4 1.5 copy.276
  415.4 1.6 copy.277
  419.3 1.5 copy.279
  421.3 1.7 copy.280
  425.4 1.5 copy.267
  426.9 12.3 %broadcast_select_fusion = (f32[384,1024]{1,0:T(8,128)}, f32[384,1024]{1,0:T(8,128)}) fusion(pred[384]{0:T(512)(128)(4,1)S(1)} %copy-done.24, bf16[1024,384]{0,1:T(8,128)(2,1)} %reduce-scatter.10.cloned.1.call-done, f32[384,1024]{1,0:T(8,128)} %bitcast.238, f32[398,1084]{1,0:T(8,128)S(1)} %maximum_convert_fusion, f32[384,1024]{1,0:T(8,128)} %bitcast.237, ...), kind=kLoop, calls=%fused_computation.135 | loop fusion | flops 14155776 | bytes 52691328 | tf_op jit(solution)/shard_map/jit(_where)/select_n | solution.py:150
  439.3 3.0 fusion.46
  442.3 15.0 %convolution_convert_fusion = bf16[2048,4096]{1,0:T(8,128)(2,1)} fusion(bf16[384,4096]{1,0:T(8,128)(2,1)} %all-gather.8.cloned.1.call-done, f32[384,2048]{1,0:T(8,128)} %get-tuple-element.63), kind=kOutput, calls=%fused_computation.1 | convolution fusion | flops 6457917440 | bytes 23068672 | tf_op jit(solution)/shard_map/dot_general | solution.py:81
  458.8 14.4 %convolution_convert_fusion.1 = bf16[4096,2048]{1,0:T(8,128)(2,1)} fusion(bf16[384,4096]{1,0:T(8,128)(2,1)} %all-gather.6.cloned.1.call-done, bf16[384,2048]{1,0:T(8,128)(2,1)S(1)} %copy-done.26), kind=kOutput, calls=%fused_computation.2 | convolution fusion | flops 6450839552 | bytes 21495808 | tf_op jit(solution)/shard_map/dot_general | solution.py:91
  473.2 10.5 %reduce-scatter.6.cloned.1.call-done = bf16[1024,384]{0,1:T(8,128)(2,1)} async-done(((bf16[4096,384]{0,1:T(8,128)(2,1)}), bf16[1024,384]{0,1:T(8,128)(2,1)}) %reduce-scatter.6.cloned.1.call-update) | async-done | bytes 786448 | tf_op jit(solution)/shard_map/reduce_scatter | solution.py:67
  483.7 2.3 fusion.41
  486.0 56.2 %all-reduce.3.cloned.1.call-done = (bf16[100,1024]{1,0:T(8,128)(2,1)}, bf16[4096,60]{0,1:T(8,128)(2,1)}) async-done(((bf16[100,1024]{1,0:T(8,128)(2,1)}, bf16[4096,60]{0,1:T(8,128)(2,1)}), (bf16[100,1024]{1,0:T(8,128)(2,1)}, bf16[4096,60]{0,1:T(8,128)(2,1)})) %all-reduce.3.cloned.1.call-update) | async-done | bytes 696336 | tf_op jit(solution)/shard_map/psum | solution.py:158
  542.2 1.7 convert_element_type.197
  543.9 2.1 convert_element_type.199
  546.0 116.0 %reduce-scatter.14.cloned.1.call-done = bf16[2048,512]{1,0:T(8,128)(2,1)} async-done(((bf16[2048,4096]{1,0:T(8,128)(2,1)}), bf16[2048,512]{1,0:T(8,128)(2,1)}) %reduce-scatter.14.cloned.1.call-update) | async-done | bytes 2097168 | tf_op jit(solution)/shard_map/reduce_scatter | solution.py:86
  662.0 4.2 convert_element_type.203
  666.2 115.3 %reduce-scatter.12.cloned.1.call-done = bf16[512,2048]{1,0:T(8,128)(2,1)} async-done(((bf16[4096,2048]{1,0:T(8,128)(2,1)}), bf16[512,2048]{1,0:T(8,128)(2,1)}) %reduce-scatter.12.cloned.1.call-update) | async-done | bytes 2097168 | tf_op jit(solution)/shard_map/reduce_scatter | solution.py:90
  781.5 4.2 convert_element_type.201
  (199 shorter events, 69.3 us)
Async XLA Ops:
  7.2 69.7 %copy-start = (bf16[4096,60]{0,1:T(8,128)(2,1)S(1)}, bf16[4096,60]{0,1:T(8,128)(2,1)}, u32[]{:S(2)}) copy-start(bf16[4096,60]{0,1:T(8,128)(2,1)} %param.12) | copy-start | bytes 1474564
  7.2 69.7 %all-gather.4.cloned.1.call-start = ((), (), s32[]{:S(2)}) async-start(), calls=%async_computation.5 | async-start | bytes 3932160 | tf_op jit(solution)/shard_map/all_gather | solution.py:48
  8.0 3.3 copy-start.23
  10.5 1.1 copy-start.2
  10.6 130.2 %all-gather.8.cloned.1.call-start = ((), (), s32[]{:S(2)}) async-start(), calls=%async_computation.8 | async-start | bytes 3932160 | tf_op jit(solution)/shard_map/all_gather | solution.py:76
  11.3 193.7 %all-gather.6.cloned.1.call-start = ((), (), s32[]{:S(2)}) async-start(), calls=%async_computation.6 | async-start | bytes 3932160 | tf_op jit(solution)/shard_map/all_gather | solution.py:60
  12.3 96.1 %collective-permute-start = (bf16[7,1024]{1,0:T(8,128)(2,1)}, bf16[7,1024]{1,0:T(8,128)(2,1)S(1)}, u32[]{:S(2)}, u32[]{:S(2)}) collective-permute-start(bf16[7,1024]{1,0:T(8,128)(2,1)} %get-tuple-element.28), channel_id=1, source_target_pairs={{0,4},{4,8},{8,12},{12,16},{16,20},{20,24},{24,28},{1,5},{5,9},{9,... | collective-permute-start | bytes 43016 | tf_op jit(solution)/shard_map/ppermute | solution.py:15
  14.6 93.8 %collective-permute-start.1 = (bf16[7,1024]{1,0:T(8,128)(2,1)}, bf16[7,1024]{1,0:T(8,128)(2,1)S(1)}, u32[]{:S(2)}, u32[]{:S(2)}) collective-permute-start(bf16[7,1024]{1,0:T(8,128)(2,1)} %get-tuple-element.29), channel_id=1, source_target_pairs={{4,0},{8,4},{12,8},{16,12},{20,16},{24,20},{28,24},{5,1},{9,5},{13... | collective-permute-start | bytes 43016 | tf_op jit(solution)/shard_map/ppermute | solution.py:18
  88.3 0.9 copy-start.20
  89.7 0.9 copy-start.18
  91.1 0.9 copy-start.16
  92.5 0.9 copy-start.14
  115.7 175.3 %reduce-scatter.8.cloned.1.call-start = ((), (), s32[]{:S(2)}) async-start(), calls=%async_computation.9 | async-start | bytes 3932160 | tf_op jit(solution)/shard_map/reduce_scatter | solution.py:99
  219.3 1.2 copy-start.25
  231.9 59.1 %copy-start.3 = (bf16[384,1024]{1,0:T(8,128)(2,1)S(1)}, bf16[384,1024]{1,0:T(8,128)(2,1)}, u32[]{:S(2)}) copy-start(bf16[384,1024]{1,0:T(8,128)(2,1)} %param.15) | copy-start | bytes 2359300
  231.9 195.0 %reduce-scatter.10.cloned.1.call-start = ((), (), s32[]{:S(2)}) async-start(), calls=%async_computation.10 | async-start | bytes 3932160 | tf_op jit(solution)/shard_map/reduce_scatter | solution.py:138
  328.7 2.1 copy-start.5
  360.2 123.5 %reduce-scatter.6.cloned.1.call-start = ((), (), s32[]{:S(2)}) async-start(), calls=%async_computation.7 | async-start | bytes 3932160 | tf_op jit(solution)/shard_map/reduce_scatter | solution.py:67
  375.0 1.1 copy-start.6
  375.0 167.2 %all-reduce.3.cloned.1.call-start = ((), (), s32[]{:S(2)}) async-start(), calls=%async_computation.13 | async-start | bytes 1474560 | tf_op jit(solution)/shard_map/psum | solution.py:158
  376.1 6.4 collective-permute-start.2
  377.6 4.9 copy-start.7
  377.6 4.9 collective-permute-start.3
  397.6 1.5 copy-start.21
  399.5 1.5 copy-start.19
  401.5 1.5 copy-start.17
  403.5 1.5 copy-start.15
  405.5 1.5 copy-start.13
  407.4 1.5 copy-start.12
  409.4 1.5 copy-start.11
  411.4 1.5 copy-start.10
  413.3 1.5 copy-start.9
  415.3 1.6 copy-start.8
  425.4 1.5 copy-start.24
  426.9 12.3 %copy-start.22 = (s32[384]{0:T(512)S(1)}, s32[384]{0:T(512)}, u32[]{:S(2)}) copy-start(s32[384]{0:T(512)} %param.10) | copy-start | bytes 4612
  442.3 219.7 %reduce-scatter.14.cloned.1.call-start = ((), (), s32[]{:S(2)}) async-start(), calls=%async_computation.12 | async-start | bytes 18874368 | tf_op jit(solution)/shard_map/reduce_scatter | solution.py:86
  457.3 1.4 copy-start.26
  457.4 324.1 %reduce-scatter.12.cloned.1.call-start = ((), (), s32[]{:S(2)}) async-start(), calls=%async_computation.11 | async-start | bytes 18874368 | tf_op jit(solution)/shard_map/reduce_scatter | solution.py:90
  473.1 10.5 %copy-start.4 = (bf16[384,1024]{1,0:T(8,128)(2,1)S(1)}, bf16[384,1024]{1,0:T(8,128)(2,1)}, u32[]{:S(2)}) copy-start(bf16[384,1024]{1,0:T(8,128)(2,1)} %fusion.44) | copy-start | bytes 2359300
  781.5 4.2 copy-start.1
Sparse Core Ops, SparseCore 0:
  10.7 66.1 all-gather.3
  78.4 62.2 all-gather.7
  142.9 62.1 all-gather.5
  232.1 58.9 reduce-scatter.7
  360.3 60.2 reduce-scatter.9
  423.3 60.2 reduce-scatter.5
  487.5 54.6 all-reduce.2
  545.8 116.1 reduce-scatter.13
  665.5 115.9 reduce-scatter.11
where the time goes:
time: 803 us; the launch traced here: 793 us
  waiting for transfers between devices  496 us (62%)
  local copies, waits for them, and re-layouts  115 us (14%)
  matrix products  96.7 us (12%)
  other arithmetic  63.2 us (8%)
  between operations  15.1 us (2%)
    reduce_scatter x1, waiting for transfers between devices, body(): lax.psum_scatter(down_term.astype(jnp.bfloat16), 'seq', scatter_dimension...  116 us
    reduce_scatter x1, waiting for transfers between devices, body(): lax.psum_scatter(lax.dot_general(full_copy, pre_grad, (((0,), (0,)), ((),...  115 us
    all_gather x1, waiting for transfers between devices, body(): full_hidden = lax.all_gather(hidden, 'tp', axis=1, tiled=True)  60.9 us
    reduce_scatter x1, waiting for transfers between devices, body(): lax.psum_scatter(lax.dot_general(up_rows, pre_grad, (((1,), (1,)), ((), (...  58.8 us
    psum x1, waiting for transfers between devices, body(): lax.psum(table_part.astype(jnp.bfloat16), 'seq').astype(jnp.float32)  56.2 us
    all_gather x1, waiting for transfers between devices, body(): shard_piece = lax.all_gather(act, 'tp', axis=1, tiled=True)  52 us
    unnamed x84, local copies, waits for them, and re-layouts  39.2 us
    mul x15, local copies, waits for them, and re-layouts, body(): act_three * padded[tap_index:tap_index + tok_rows]  36.6 us
  transfers between devices with their start and end apart: 13, of which 8 were waited for; matrix products, arithmetic and copies ran while one was open for 21% of the time, Pallas kernels for 0%

commit v1 on v0

v1 whole, which is shorter than its diff:
```python
import jax
import jax.numpy as jnp
from jax import lax
from jax.sharding import PartitionSpec as P

KW = 15
SENT = 100


def halo(low_edge, high_edge):
    count = lax.axis_size("seq")
    forward = [(i, i + 1) for i in range(count - 1)]
    backward = [(target, source) for source, target in forward]
    low = lax.ppermute(high_edge, "seq", forward)
    high = lax.ppermute(low_edge, "seq", backward)
    return low, high


def gelu_tanh(values):
    return jax.nn.gelu(values, approximate=True)


def dot(a, b, dims=((1,), (0,))):
    return lax.dot_general(a, b, (dims, ((), ())), preferred_element_type=jnp.float32)


def turned(block, shift):
    count = lax.axis_size("tp")
    return lax.ppermute(block, "tp", [(i, (i + shift) % count) for i in range(count)])


def swapped(block, bit):
    count = lax.axis_size("seq")
    return lax.ppermute(block, "seq", [(i, i ^ (1 << bit)) for i in range(count)])


def my_bit(bit):
    return (lax.axis_index("seq") // (1 << bit)) % 2


def scatter_sum(pieces, bits, order):
    bits = list(bits)
    for bit in order:
        axis = bits.index(bit)
        bits.pop(axis)
        mine = my_bit(bit)

        def part(which):
            total = 0.0
            for piece in pieces:
                total = total + lax.dynamic_index_in_dim(
                    piece, which, axis, keepdims=False
                ).astype(jnp.float32)
            return total.astype(jnp.bfloat16)

        pieces = [part(mine), swapped(part(1 - mine), bit)]
    return pieces[0].astype(jnp.float32) + pieces[1].astype(jnp.float32)


def seq_bits():
    return lax.axis_size("seq").bit_length() - 1


def weight_grad(features, factor):
    count, depth = seq_bits(), features.shape[0]
    rows = features.shape[1] >> count
    grouped = features.reshape(depth, 1 << (count - 1), 2, rows)
    width = factor.shape[1]

    def half(which, factor):
        chosen = lax.dynamic_index_in_dim(grouped, which, 2, keepdims=False)
        return dot(chosen.reshape(depth, -1), factor, ((0,), (0,))).astype(jnp.bfloat16)

    mine = my_bit(0)
    sent = half(1 - mine, factor)
    sent, factor = lax.optimization_barrier((sent, factor))
    got = swapped(sent, 0)
    kept = half(mine, factor)
    shape = (2,) * (count - 1) + (2, rows // 2, width)
    bits = list(range(count - 1, 0, -1))
    pieces = [kept.reshape(shape), got.reshape(shape)]
    lead = len(bits)
    upper = scatter_sum([lax.index_in_dim(p, 0, lead, False) for p in pieces], bits, bits)
    lower = scatter_sum([lax.index_in_dim(p, 1, lead, False) for p in pieces], bits, bits[::-1])
    return jnp.concatenate([upper, lower], axis=0)


def seq_sum(values):
    def step(block, bit):
        other = swapped(block, bit)
        return (block.astype(jnp.float32) + other.astype(jnp.float32)).astype(jnp.bfloat16)

    values = step(values, 0)
    cut = values.shape[0] // 2 // 16 * 16
    first, second = values[:cut], values[cut:]
    bits = list(range(1, seq_bits()))
    for one, two in zip(bits, bits[::-1]):
        first, second = step(first, one), step(second, two)
    return jnp.concatenate([first, second], axis=0)


def body(
    embeddings,
    span_mask,
    sentinel_id,
    sentinel_table,
    gen_weight,
    up_weight,
    down_weight,
    cotangent,
):
    bf16, f32 = jnp.bfloat16, jnp.float32
    tok_rows, feat_width = embeddings.shape
    gen_cols = gen_weight.shape[1]
    head_count = gen_cols // KW
    head_width = feat_width // head_count
    reach = (KW - 1) // 2
    tp_count, tp_index = lax.axis_size("tp"), lax.axis_index("tp")
    sentinel_codes = jnp.arange(SENT, dtype=jnp.int32)
    onehot = sentinel_id[:, None] == sentinel_codes[None, :]
    picked = dot(onehot.astype(bf16), sentinel_table).astype(bf16)
    masked = span_mask[:, None] == 1
    hidden = jnp.where(masked, picked, embeddings)

    gen_blocks = []
    for shift in range(tp_count):
        start = (tp_index + shift) % tp_count * feat_width
        rows = lax.dynamic_slice_in_dim(gen_weight, start, feat_width, axis=0)
        gen_blocks.append(turned(rows, shift) if shift else rows)
    gen_rows = jnp.concatenate(gen_blocks, axis=1)
    partial = dot(hidden, gen_rows)
    logits = partial[:, :gen_cols]
    for shift in range(1, tp_count):
        logits = logits + turned(partial[:, shift * gen_cols : (shift + 1) * gen_cols], -shift)
    exp_logits = jnp.exp(logits)
    kernels = []
    for head in range(head_count):
        taps = exp_logits[:, head * KW : (head + 1) * KW]
        kernels.append(taps / jnp.sum(taps, axis=-1, keepdims=True))

    low, high = halo(hidden[:reach], hidden[tok_rows - reach :])
    padded = jnp.concatenate([low, hidden, high], axis=0)
    long_rows = tok_rows + 2 * reach
    ahead = jnp.arange(long_rows)[None, :] - jnp.arange(tok_rows)[:, None]
    conv = []
    for head in range(head_count):
        columns = slice(head * head_width, (head + 1) * head_width)
        band = jnp.zeros((tok_rows, long_rows), f32)
        for tap in range(KW):
            band = jnp.where(ahead == tap, kernels[head][:, tap : tap + 1], band)
        conv.append(dot(band.astype(bf16), padded[:, columns]))
    act = (hidden.astype(f32) + jnp.concatenate(conv, axis=1)).astype(bf16)

    full_cot = lax.all_gather(cotangent, "tp", axis=1, tiled=True)
    full_act = lax.all_gather(act, "tp", axis=1, tiled=True)
    middle_grad = dot(full_cot, down_weight, ((1,), (1,)))
    pre_sum = dot(full_act, up_weight)
    middle, gelu_back = jax.vjp(gelu_tanh, pre_sum)
    middle = middle.astype(bf16)
    pre_grad = gelu_back(middle_grad)[0].astype(bf16)

    back_part = dot(up_weight, pre_grad, ((1,), (1,))).astype(bf16)
    back_part, middle, pre_grad = lax.optimization_barrier((back_part, middle, pre_grad))
    act_back = lax.psum_scatter(back_part, "tp", scatter_dimension=0, tiled=True)
    down_grad = weight_grad(full_cot, middle).T
    up_grad = weight_grad(full_act, pre_grad)
    ffn_part = dot(down_weight, middle, ((0,), (1,))).astype(bf16)
    ffn_total = lax.psum_scatter(ffn_part, "tp", scatter_dimension=0, tiled=True)
    layer_output = (act.astype(f32) + ffn_total.astype(f32).T).astype(bf16)

    act_grad = cotangent.astype(f32) + act_back.astype(f32).T
    short_grad = act_grad.astype(bf16)
    kernel_short = jnp.concatenate(kernels, axis=1).astype(bf16)
    joined = jnp.concatenate([short_grad, kernel_short], axis=1)
    low, high = halo(joined[:reach], joined[tok_rows - reach :])
    grad_pad = jnp.concatenate([low[:, :feat_width], short_grad, high[:, :feat_width]], axis=0)
    kernel_pad = jnp.concatenate([low[:, feat_width:], kernel_short, high[:, feat_width:]], axis=0)
    logit_grads = []
    for head in range(head_count):
        columns = slice(head * head_width, (head + 1) * head_width)
        scores = dot(short_grad[:, columns], padded[:, columns], ((1,), (1,)))
        kernel_grad = jnp.stack(
            [jnp.sum(jnp.where(ahead == tap, scores, 0.0), axis=-1) for tap in range(KW)], axis=-1
        )
        weighted = jnp.sum(kernels[head] * kernel_grad, axis=-1, keepdims=True)
        logit_grads.append((kernels[head] * (kernel_grad - weighted)).astype(bf16))
    logit_grad = jnp.concatenate(logit_grads, axis=1)
    logit_grads = jnp.concatenate(
        [logit_grad] + [turned(logit_grad, shift) for shift in range(1, tp_count)], axis=1
    )

    behind = jnp.arange(tok_rows)[None, :] - jnp.arange(long_rows)[:, None] + 2 * reach
    conv_back = []
    for head in range(head_count):
        columns = slice(head * head_width, (head + 1) * head_width)
        band = jnp.zeros((long_rows, tok_rows), f32)
        for tap in range(KW):
            place = head * KW + tap
            band = jnp.where(behind == tap, kernel_pad[:, place : place + 1].astype(f32), band)
        conv_back.append(dot(band.astype(bf16), grad_pad[:, columns], ((0,), (0,))))

    gen_part = dot(logit_grads, hidden, ((0,), (0,))).astype(bf16)
    gen_owned = [gen_part[:gen_cols]]
    for shift in range(1, tp_count):
        gen_owned.append(turned(gen_part[shift * gen_cols : (shift + 1) * gen_cols], -shift))
    gen_back = dot(logit_grads, gen_rows, ((1,), (1,)))
    hidden_grad = act_grad + jnp.concatenate(conv_back, axis=1) + gen_back
    embed_grad = jnp.where(masked, f32(0.0), hidden_grad)
    table_part = dot(
        onehot.astype(bf16), jnp.where(masked, hidden_grad, f32(0.0)).astype(bf16), ((0,), (0,))
    ).astype(bf16)
    summed = seq_sum(jnp.concatenate(gen_owned + [table_part], axis=0))
    gen_total = tp_count * gen_cols
    table_grad = summed[gen_total:].astype(f32)
    gen_sum = summed[:gen_total].reshape(tp_count, gen_cols, feat_width)
    gen_sum = lax.dynamic_slice_in_dim(
        jnp.concatenate([gen_sum, gen_sum], axis=0), (tp_count - tp_index) % tp_count, tp_count, axis=0
    )
    gen_sum = gen_sum.transpose(0, 2, 1).reshape(tp_count * feat_width, gen_cols).astype(f32)
    return (layer_output, embed_grad, table_grad, gen_sum, up_grad, down_grad)


def solution(mesh):
    placed = (
        P("seq", "tp"),
        P("seq"),
        P("seq"),
        P(None, "tp"),
        P(None, "tp"),
        P(None, "tp"),
        P("tp", None),
        P("seq", "tp"),
    )
    return jax.shard_map(
        body,
        mesh=mesh,
        in_specs=placed,
        out_specs=(
            P("seq", "tp"),
            P("seq", "tp"),
            P(None, "tp"),
            P(None, "tp"),
            P("seq", "tp"),
            P("tp", "seq"),
        ),
        check_vma=False,
    )
```

time: 803 us -> 539 us (0.67)
  waiting for transfers between devices: 496 us -> 200 us
  starting transfers between devices: 7.48 us -> 49.5 us
  other arithmetic: 63.2 us -> 54.8 us
    reduce_scatter x5 -> x2, waiting for transfers between devices: 301 us -> 7.97 us  [the longest x1 7.97 us: body(): lax.psum_scatter(back_part, 'tp', scatter_dimension=0, tiled=True)]
    ppermute x4 -> x31, waiting for transfers between devices: 0.01 us -> 107 us  [the longest x15 76.8 us: swapped(): return lax.ppermute(block, 'seq', [(i, i ^ 1 << bit) for i in range(count)])]
    mul x75 -> x0, local copies, waits for them, and re-layouts: 71.5 us -> none  [the longest x15 36.6 us: body(): act_three * padded[tap_index:tap_index + tok_rows]]
    psum x1 -> x0, waiting for transfers between devices: 56.2 us -> none  [body(): lax.psum(table_part.astype(jnp.bfloat16), 'seq').astype(jnp.float32)]
    all_gather x3 -> x2, waiting for transfers between devices: 138 us -> 85.2 us  [the longest x1 53.7 us: body(): full_act = lax.all_gather(act, 'tp', axis=1, tiled=True)]
    ppermute x4 -> x31, starting transfers between devices: 6.69 us -> 49.1 us  [the longest x12 24.8 us: turned(): lax.ppermute(block, 'tp', [(i, (i + shift) % count) for i in range(count)])]
    slice x5 -> x18, local copies, waits for them, and re-layouts: 2.24 us -> 25.8 us  [the longest x4 20.2 us: weight_grad(): lax.index_in_dim(p, 0, lead, False)]
    convert_element_type x7 -> x22, other arithmetic: 22 us -> 40.3 us  [the longest x10 26.5 us: part(): return total.astype(jnp.bfloat16)]
  transfers between devices with their start and end apart: 13 -> 35, of which waited for: 8 -> 14; matrix products, arithmetic and copies ran while one was open for 21% -> 43% of each run, Pallas kernels for 0% -> 0%
where the time goes in v1:
time: 539 us; the launch traced here: 532 us
  waiting for transfers between devices  200 us (37%)
  local copies, waits for them, and re-layouts  113 us (21%)
  matrix products  99.1 us (18%)
  other arithmetic  54.8 us (10%)
  starting transfers between devices  49.5 us (9%)
  between operations  15.7 us (3%)
    dot_general x25, matrix products, dot(): lax.dot_general(a, b, (dims, ((), ())), preferred_element_type=jnp.float32)  99.1 us
    ppermute x15, waiting for transfers between devices, swapped(): return lax.ppermute(block, 'seq', [(i, i ^ 1 << bit) for i in range(count)])  76.8 us
    all_gather x1, waiting for transfers between devices, body(): full_act = lax.all_gather(act, 'tp', axis=1, tiled=True)  53.7 us
    unnamed x136, local copies, waits for them, and re-layouts  43.5 us
    all_gather x1, waiting for transfers between devices, body(): full_cot = lax.all_gather(cotangent, 'tp', axis=1, tiled=True)  31.4 us
    ppermute x12, waiting for transfers between devices, turned(): lax.ppermute(block, 'tp', [(i, (i + shift) % count) for i in range(count)])  30.4 us
    convert_element_type x10, other arithmetic, part(): return total.astype(jnp.bfloat16)  26.5 us
    ppermute x12, starting transfers between devices, turned(): lax.ppermute(block, 'tp', [(i, (i + shift) % count) for i in range(count)])  24.8 us
  transfers between devices with their start and end apart: 35, of which 14 were waited for; matrix products, arithmetic and copies ran while one was open for 43% of the time, Pallas kernels for 0%

profile of v1, /device:TPU:0, one launch (start us, length us, event | category | flops | bytes accessed | tf_op | source)
XLA Modules:
  0.0 532.5 jit_solution(14169242515913191193)
XLA Ops:
  7.2 2.4 copy.223
  9.8 5.1 collective-permute-start.2
  18.3 3.0 collective-permute-start.6
  21.4 10.9 %collective-permute-done.1 = bf16[1024,60]{0,1:T(8,128)(2,1)S(1)} collective-permute-done((bf16[1024,60]{0,1:T(8,128)(2,1)S(1)}, bf16[1024,60]{0,1:T(8,128)(2,1)S(1)}, u32[]{:S(2)}, u32[]{:S(2)}) %collective-permute-start.1) | collective-permute-done | bytes 122912 | tf_op jit(solution)/shard_map/ppermute | solution.py:29
  32.8 5.7 %collective-permute-start.5 = (f32[384,60]{0,1:T(8,128)S(1)}, f32[384,60]{0,1:T(8,128)S(1)}, u32[]{:S(2)}, u32[]{:S(2)}) collective-permute-start(f32[384,60]{0,1:T(8,128)S(1)} %get-tuple-element.197), channel_id=1, source_target_pairs={{0,1},{1,2},{2,3},{3,0},{4,5},{5,6},{6,7},{7,4},{8,9},{9,10},{10,1... | collective-permute-start | bytes 276488 | tf_op jit(solution)/shard_map/ppermute | solution.py:29
  38.5 2.0 collective-permute-start.4
  40.5 2.8 collective-permute-start.3
  44.0 6.8 %collective-permute-done.4 = f32[384,60]{0,1:T(8,128)S(1)} collective-permute-done((f32[384,60]{0,1:T(8,128)S(1)}, f32[384,60]{0,1:T(8,128)S(1)}, u32[]{:S(2)}, u32[]{:S(2)}) %collective-permute-start.4) | collective-permute-done | bytes 92192 | tf_op jit(solution)/shard_map/ppermute | solution.py:29
  54.4 31.4 %all-gather.3.cloned.1.call-done = bf16[384,4096]{0,1:T(8,128)(2,1)} async-done(((bf16[384,1024]{0,1:T(8,128)(2,1)}), bf16[384,4096]{0,1:T(8,128)(2,1)}) %all-gather.3.cloned.1.call-update) | async-done | bytes 3145744 | tf_op jit(solution)/shard_map/all_gather | solution.py:154
  85.9 12.4 %fusion.370 = f32[384,2048]{1,0:T(8,128)} fusion(bf16[384,4096]{0,1:T(8,128)(2,1)} %all-gather.3.cloned.1.call-done, bf16[2048,4096]{1,0:T(8,128)(2,1)} %param.14), kind=kOutput, calls=%fused_computation.650 | convolution fusion | flops 6442450944 | bytes 23068672 | tf_op jit(solution)/shard_map/dot_general | solution.py:24
  98.2 53.7 %all-gather.5.cloned.1.call-done = bf16[384,4096]{0,1:T(8,128)(2,1)} async-done(((bf16[384,1024]{0,1:T(8,128)(2,1)}), bf16[384,4096]{0,1:T(8,128)(2,1)}) %all-gather.5.cloned.1.call-update) | async-done | bytes 3145744 | tf_op jit(solution)/shard_map/all_gather | solution.py:155
  152.0 14.4 %multiply_convert_fusion = (bf16[384,2048]{1,0:T(8,128)(2,1)}, bf16[384,2048]{1,0:T(8,128)(2,1)S(1)}) fusion(f32[384,2048]{1,0:T(8,128)} %fusion.370, bf16[384,4096]{0,1:T(8,128)(2,1)} %all-gather.5.cloned.1.call-done, bf16[4096,2048]{1,0:T(8,128)(2,1)} %param.13), kind=kOutput, calls=%fused_computation.27 | convolution fusion | flops 6459752448 | bytes 26214400 | tf_op jit(solution)/shard_map/dot_general | solution.py:24
  167.5 13.6 %fusion = bf16[4096,384]{1,0:T(8,128)(2,1)} fusion(bf16[384,2048]{1,0:T(8,128)(2,1)S(1)} %get-tuple-element.16, bf16[4096,2048]{1,0:T(8,128)(2,1)} %param.13), kind=kOutput, calls=%fused_computation.6 | convolution fusion | flops 6444023808 | bytes 21495808 | tf_op jit(solution)/shard_map/dot_general | solution.py:24
  181.4 3.8 constant_dynamic-slice_fusion.5
  185.2 7.2 %convolution_convert_fusion.3 = bf16[2048,2048]{1,0:T(8,128)(2,1)} fusion(bf16[384,2048]{0,1:T(8,128)(2,1)S(1)} %bitcast.189, bf16[384,2048]{1,0:T(8,128)(2,1)S(1)} %copy-done.59), kind=kOutput, calls=%fused_computation.3 | convolution fusion | flops 3225419776 | bytes 11534336 | tf_op jit(solution)/shard_map/dot_general | solution.py:24
  192.4 6.8 %convolution_convert_fusion.1 = bf16[2048,2048]{1,0:T(8,128)(2,1)} fusion(bf16[384,2048]{0,1:T(8,128)(2,1)S(1)} %bitcast.188, bf16[384,2048]{1,0:T(8,128)(2,1)S(1)} %copy-done.60), kind=kOutput, calls=%fused_computation.1 | convolution fusion | flops 3225419776 | bytes 11534336 | tf_op jit(solution)/shard_map/dot_general | solution.py:24
  199.7 4.7 convolution_convert_fusion
  204.5 3.9 fusion.362
  208.4 13.7 %fusion.1 = bf16[4096,384]{1,0:T(8,128)(2,1)} fusion(bf16[384,2048]{1,0:T(8,128)(2,1)S(1)} %copy-done.60, bf16[2048,4096]{1,0:T(8,128)(2,1)} %param.14), kind=kOutput, calls=%fused_computation.7 | convolution fusion | flops 6444023808 | bytes 21495808 | tf_op jit(solution)/shard_map/dot_general | solution.py:24
  222.2 8.4 %convolution_convert_fusion.2 = bf16[2048,2048]{1,0:T(8,128)(2,1)} fusion(bf16[384,2048]{0,1:T(8,128)(2,1)S(1)} %bitcast.186, bf16[384,2048]{1,0:T(8,128)(2,1)} %copy-done.58), kind=kOutput, calls=%fused_computation.2 | convolution fusion | flops 3225419776 | bytes 11534336 | tf_op jit(solution)/shard_map/dot_general | solution.py:24
  230.5 1.8 constant_dynamic-slice_fusion.6
  232.3 8.0 %reduce-scatter.5.cloned.1.call-done = bf16[1024,384]{1,0:T(8,128)(2,1)} async-done(((bf16[4096,384]{1,0:T(8,128)(2,1)}), bf16[1024,384]{1,0:T(8,128)(2,1)}) %reduce-scatter.5.cloned.1.call-update) | async-done | bytes 786448 | tf_op jit(solution)/shard_map/reduce_scatter | solution.py:164
  244.6 8.9 %concatenate.51 = bf16[384,1084]{0,1:T(8,128)(2,1)} concatenate(bf16[384,1024]{0,1:T(8,128)(2,1)} %copy-done.12, bf16[384,15]{0,1:T(8,128)(2,1)S(1)} %get-tuple-element.156, bf16[384,15]{0,1:T(8,128)(2,1)S(1)} %get-tuple-element.201, bf16[384,15]{0,1:T(8,128)(2,1)S(1)} %get-tuple-element.203, bf16[384,15]{0,1:T(8,128)(2,1)S(1)} %get-tuple-element.199), dimensions={1} | concatenate | bytes 1665024 | tf_op jit(solution)/shard_map/concatenate | solution.py:174
  270.3 3.8 collective-permute-start.8
  281.6 2.8 collective-permute-start.12
  286.9 1.8 fusion.74
  288.7 1.8 fusion.73
  290.5 1.8 fusion.72
  292.3 1.8 fusion.71
  295.4 2.5 concatenate.57
  299.3 1.9 collective-permute-start.15
  301.3 3.0 broadcast_select_fusion
  306.5 10.9 %collective-permute-done.14 = bf16[60,1024]{1,0:T(8,128)(2,1)S(1)} collective-permute-done((bf16[60,1024]{1,0:T(8,128)(2,1)S(1)}, bf16[60,1024]{1,0:T(8,128)(2,1)S(1)}, u32[]{:S(2)}, u32[]{:S(2)}) %collective-permute-start.14) | collective-permute-done | bytes 122912 | tf_op jit(solution)/shard_map/ppermute | solution.py:29
  318.7 3.0 concatenate.58
  321.8 6.7 %fusion.364 = (bf16[2,2,1,256,2048]{4,3,2,1,0:T(8,128)(2,1)}, bf16[2,2,1,256,2048]{4,3,2,1,0:T(8,128)(2,1)}) fusion(bf16[2,2,2,256,2048]{4,3,2,1,0:T(8,128)(2,1)} %bitcast.180), kind=kLoop, calls=%fused_computation.644 | loop fusion | bytes 16777216 | tf_op jit(solution)/shard_map/slice | solution.py:83
  333.8 2.5 constant_dynamic-slice_fusion.3
  336.3 4.0 copy.253
  340.2 2.5 copy.250
  342.8 3.9 copy.247
  346.7 2.8 copy.244
  349.6 2.0 add_convert_fusion.12
  354.0 2.2 fusion.23
  356.2 2.3 copy.235
  358.5 3.0 copy.236
  369.4 4.2 fusion.365
  374.0 4.3 add_convert_fusion.5
  379.1 4.3 add_convert_fusion.7
  384.9 5.3 %fusion.363 = (bf16[2,2,1,256,2048]{4,3,2,1,0:T(8,128)(2,1)}, bf16[2,2,1,256,2048]{4,3,2,1,0:T(8,128)(2,1)S(1)}) fusion(bf16[2,2,2,256,2048]{4,3,2,1,0:T(8,128)(2,1)} %bitcast.84), kind=kLoop, calls=%fused_computation.643 | loop fusion | bytes 16777216 | tf_op jit(solution)/shard_map/slice | solution.py:83
  390.2 2.4 constant_dynamic-slice_fusion.1
  392.7 4.2 copy.254
  396.8 4.2 fusion.12
  402.5 2.5 constant_dynamic-slice_fusion.2
  405.1 4.0 copy.248
  409.0 4.1 fusion.11
  414.3 3.9 copy.252
  418.2 4.0 copy.246
  422.2 2.9 add_convert_fusion.1
  425.1 2.2 collective-permute-done.24
  435.8 36.4 %collective-permute-done.29 = bf16[2,256,2048]{1,2,0:T(8,128)(2,1)} collective-permute-done((bf16[2,256,2048]{1,2,0:T(8,128)(2,1)}, bf16[2,256,2048]{1,2,0:T(8,128)(2,1)}, u32[]{:S(2)}, u32[]{:S(2)}) %collective-permute-start.29) | collective-permute-done | bytes 2097184 | tf_op jit(solution)/shard_map/ppermute | solution.py:34
  475.4 1.9 collective-permute-done.27
  480.1 19.5 %collective-permute-done.25 = bf16[256,2048]{1,0:T(8,128)(2,1)S(1)} collective-permute-done((bf16[256,2048]{1,0:T(8,128)(2,1)S(1)}, bf16[256,2048]{1,0:T(8,128)(2,1)S(1)}, u32[]{:S(2)}, u32[]{:S(2)}) %collective-permute-start.25) | collective-permute-done | bytes 1048608 | tf_op jit(solution)/shard_map/ppermute | solution.py:34
  503.1 2.3 pad_maximum_fusion
  505.4 14.4 %collective-permute-done.30 = bf16[256,2048]{0,1:T(8,128)(2,1)S(1)} collective-permute-done((bf16[256,2048]{0,1:T(8,128)(2,1)S(1)}, bf16[256,2048]{0,1:T(8,128)(2,1)S(1)}, u32[]{:S(2)}, u32[]{:S(2)}) %collective-permute-start.30) | collective-permute-done | bytes 1048608 | tf_op jit(solution)/shard_map/ppermute | solution.py:34
  522.9 2.6 maximum_bitcast_fusion
  (309 shorter events, 88.6 us)
Async XLA Ops:
  7.2 9.2 %copy-start = (bf16[100,1024]{1,0:T(8,128)(2,1)S(1)}, bf16[100,1024]{1,0:T(8,128)(2,1)}, u32[]{:S(2)}) copy-start(bf16[100,1024]{1,0:T(8,128)(2,1)} %param.11) | copy-start | bytes 614404
  7.2 8.8 %copy-start.20 = (bf16[384,1024]{1,0:T(8,128)(2,1)S(1)}, bf16[384,1024]{1,0:T(8,128)(2,1)}, u32[]{:S(2)}) copy-start(bf16[384,1024]{1,0:T(8,128)(2,1)} %param.8) | copy-start | bytes 2359300
  7.2 78.7 %all-gather.3.cloned.1.call-start = ((), (), s32[]{:S(2)}) async-start(), calls=%async_computation.2 | async-start | bytes 3932160 | tf_op jit(solution)/shard_map/all_gather | solution.py:154
  9.6 6.7 %copy-start.38 = (s32[384]{0:T(512)S(1)}, s32[384]{0:T(512)}, u32[]{:S(2)}) copy-start(s32[384]{0:T(512)} %param.9) | copy-start | bytes 4612
  9.6 6.7 %copy-start.34 = (s32[384]{0:T(512)S(1)}, s32[384]{0:T(512)}, u32[]{:S(2)}) copy-start(s32[384]{0:T(512)} %param.10) | copy-start | bytes 4612
  9.7 142.3 %all-gather.5.cloned.1.call-start = ((), (), s32[]{:S(2)}) async-start(), calls=%async_computation.3 | async-start | bytes 3932160 | tf_op jit(solution)/shard_map/all_gather | solution.py:155
  9.8 11.5 %collective-permute-start.2 = (bf16[1024,60]{0,1:T(8,128)(2,1)S(1)}, bf16[1024,60]{0,1:T(8,128)(2,1)S(1)}, u32[]{:S(2)}, u32[]{:S(2)}) collective-permute-start(bf16[1024,60]{0,1:T(8,128)(2,1)S(1)} %get-tuple-element.190), channel_id=1, source_target_pairs={{0,3},{1,0},{2,1},{3,2},{4,7},{5,4},{6,5},{7,6},{8,11},{9,8},{10,9... | collective-permute-start | bytes 368648 | tf_op jit(solution)/shard_map/ppermute | solution.py:29
  14.9 17.4 %collective-permute-start.1 = (bf16[1024,60]{0,1:T(8,128)(2,1)S(1)}, bf16[1024,60]{0,1:T(8,128)(2,1)S(1)}, u32[]{:S(2)}, u32[]{:S(2)}) collective-permute-start(bf16[1024,60]{0,1:T(8,128)(2,1)S(1)} %get-tuple-element.191), channel_id=1, source_target_pairs={{0,2},{1,3},{2,0},{3,1},{4,6},{5,7},{6,4},{7,5},{8,10},{9,11},{10,... | collective-permute-start | bytes 368648 | tf_op jit(solution)/shard_map/ppermute | solution.py:29
  14.9 17.4 %collective-permute-start = (bf16[1024,60]{0,1:T(8,128)(2,1)S(1)}, bf16[1024,60]{0,1:T(8,128)(2,1)S(1)}, u32[]{:S(2)}, u32[]{:S(2)}) collective-permute-start(bf16[1024,60]{0,1:T(8,128)(2,1)S(1)} %get-tuple-element.189), channel_id=1, source_target_pairs={{0,1},{1,2},{2,3},{3,0},{4,5},{5,6},{6,7},{7,4},{8,9},{9,10},{10,1... | collective-permute-start | bytes 368648 | tf_op jit(solution)/shard_map/ppermute | solution.py:29
  16.4 16.4 %copy-start.36 = (pred[384]{0:T(512)(128)(4,1)}, pred[384]{0:T(512)(128)(4,1)S(1)}, u32[]{:S(2)}) copy-start(pred[384]{0:T(512)(128)(4,1)S(1)} %broadcast_compare_fusion) | copy-start | bytes 1156
  17.0 26.3 %collective-permute-start.7 = (bf16[7,1024]{0,1:T(8,128)(2,1)S(1)}, bf16[7,1024]{0,1:T(8,128)(2,1)S(1)}, u32[]{:S(2)}, u32[]{:S(2)}) collective-permute-start(bf16[7,1024]{0,1:T(8,128)(2,1)S(1)} %get-tuple-element.187), channel_id=1, source_target_pairs={{4,0},{8,4},{12,8},{16,12},{20,16},{24,20},{28,24},{5,1},{9,5},{13... | collective-permute-start | bytes 43016 | tf_op jit(solution)/shard_map/ppermute | solution.py:15
  18.3 25.0 %collective-permute-start.6 = (bf16[7,1024]{0,1:T(8,128)(2,1)S(1)}, bf16[7,1024]{0,1:T(8,128)(2,1)S(1)}, u32[]{:S(2)}, u32[]{:S(2)}) collective-permute-start(bf16[7,1024]{0,1:T(8,128)(2,1)S(1)} %get-tuple-element.186), channel_id=1, source_target_pairs={{0,4},{4,8},{8,12},{12,16},{16,20},{20,24},{24,28},{1,5},{5,9},{9,... | collective-permute-start | bytes 43016 | tf_op jit(solution)/shard_map/ppermute | solution.py:14
  21.4 22.6 %copy-start.51 = (bf16[1024,60]{0,1:T(8,128)(2,1)}, bf16[1024,60]{0,1:T(8,128)(2,1)S(1)}, u32[]{:S(2)}) copy-start(bf16[1024,60]{0,1:T(8,128)(2,1)S(1)} %collective-permute-done.2) | copy-start | bytes 368644
  32.3 11.7 %copy-start.53 = (bf16[1024,60]{0,1:T(8,128)(2,1)}, bf16[1024,60]{0,1:T(8,128)(2,1)S(1)}, u32[]{:S(2)}) copy-start(bf16[1024,60]{0,1:T(8,128)(2,1)S(1)} %collective-permute-done.1) | copy-start | bytes 368644
  32.3 11.7 %copy-start.55 = (bf16[1024,60]{0,1:T(8,128)(2,1)}, bf16[1024,60]{0,1:T(8,128)(2,1)S(1)}, u32[]{:S(2)}) copy-start(bf16[1024,60]{0,1:T(8,128)(2,1)S(1)} %collective-permute-done) | copy-start | bytes 368644
  32.8 11.2 %collective-permute-start.5 = (f32[384,60]{0,1:T(8,128)S(1)}, f32[384,60]{0,1:T(8,128)S(1)}, u32[]{:S(2)}, u32[]{:S(2)}) collective-permute-start(f32[384,60]{0,1:T(8,128)S(1)} %get-tuple-element.197), channel_id=1, source_target_pairs={{0,1},{1,2},{2,3},{3,0},{4,5},{5,6},{6,7},{7,4},{8,9},{9,10},{10,1... | collective-permute-start | bytes 276488 | tf_op jit(solution)/shard_map/ppermute | solution.py:29
  38.5 12.4 %collective-permute-start.4 = (f32[384,60]{0,1:T(8,128)S(1)}, f32[384,60]{0,1:T(8,128)S(1)}, u32[]{:S(2)}, u32[]{:S(2)}) collective-permute-start(f32[384,60]{0,1:T(8,128)S(1)} %get-tuple-element.198), channel_id=1, source_target_pairs={{0,2},{1,3},{2,0},{3,1},{4,6},{5,7},{6,4},{7,5},{8,10},{9,11},{10,... | collective-permute-start | bytes 276488 | tf_op jit(solution)/shard_map/ppermute | solution.py:29
  40.5 10.4 %collective-permute-start.3 = (f32[384,60]{0,1:T(8,128)S(1)}, f32[384,60]{0,1:T(8,128)S(1)}, u32[]{:S(2)}, u32[]{:S(2)}) collective-permute-start(f32[384,60]{0,1:T(8,128)S(1)} %get-tuple-element.196), channel_id=1, source_target_pairs={{0,3},{1,0},{2,1},{3,2},{4,7},{5,4},{6,5},{7,6},{8,11},{9,8},{10,9... | collective-permute-start | bytes 276488 | tf_op jit(solution)/shard_map/ppermute | solution.py:29
  44.0 8.6 %copy-start.18 = (bf16[398,1024]{0,1:T(8,128)(2,1)}, bf16[398,1024]{0,1:T(8,128)(2,1)S(1)}, u32[]{:S(2)}) copy-start(bf16[398,1024]{0,1:T(8,128)(2,1)S(1)} %pad_maximum_fusion.1) | copy-start | bytes 2445316
  54.2 186.1 %reduce-scatter.5.cloned.1.call-start = ((), (), s32[]{:S(2)}) async-start(), calls=%async_computation.5 | async-start | bytes 3932160 | tf_op jit(solution)/shard_map/reduce_scatter | solution.py:164
  181.2 172.8 %reduce-scatter.3.cloned.1.call-start = ((), (), s32[]{:S(2)}) async-start(), calls=%async_computation.4 | async-start | bytes 3932160 | tf_op jit(solution)/shard_map/reduce_scatter | solution.py:168
  185.2 7.2 %copy-start.60 = (bf16[384,2048]{1,0:T(8,128)(2,1)S(1)}, bf16[384,2048]{1,0:T(8,128)(2,1)}, u32[]{:S(2)}) copy-start(bf16[384,2048]{1,0:T(8,128)(2,1)} %get-tuple-element.18) | copy-start | bytes 4718596
  192.4 176.9 %collective-permute-start.21 = (bf16[2048,2048]{1,0:T(8,128)(2,1)}, bf16[2048,2048]{1,0:T(8,128)(2,1)}, u32[]{:S(2)}, u32[]{:S(2)}) collective-permute-start(bf16[2048,2048]{1,0:T(8,128)(2,1)} %convolution_convert_fusion.3), channel_id=1, source_target_pairs={{0,4},{4,0},{8,12},{12,8},{16,20},{20,16},{24,28},{28,24},{1,5},{5... | collective-permute-start | bytes 25165832 | tf_op jit(solution)/shard_map/ppermute | solution.py:34
  199.2 185.7 %collective-permute-start.26 = (bf16[2048,2048]{1,0:T(8,128)(2,1)}, bf16[2048,2048]{1,0:T(8,128)(2,1)}, u32[]{:S(2)}, u32[]{:S(2)}) collective-permute-start(bf16[2048,2048]{1,0:T(8,128)(2,1)} %convolution_convert_fusion.1), channel_id=1, source_target_pairs={{0,4},{4,0},{8,12},{12,8},{16,20},{20,16},{24,28},{28,24},{1,5},{5... | collective-permute-start | bytes 25165832 | tf_op jit(solution)/shard_map/ppermute | solution.py:34
  222.1 8.4 %copy-start.5 = (bf16[2,2,1,256,2048]{4,3,2,1,0:T(8,128)(2,1)S(1)}, bf16[2,2,1,256,2048]{4,3,2,1,0:T(8,128)(2,1)}, u32[]{:S(2)}) copy-start(bf16[2,2,1,256,2048]{4,3,2,1,0:T(8,128)(2,1)} %get-tuple-element.159) | copy-start | bytes 12582916
  253.8 5.1 copy-start.41
  253.8 5.6 %copy-start.40 = (f32[384]{0:T(512)S(1)}, f32[384]{0:T(512)}, u32[]{:S(2)}) copy-start(f32[384]{0:T(512)} %get-tuple-element.27) | copy-start | bytes 4612
  253.8 6.1 %copy-start.39 = (f32[384]{0:T(512)S(1)}, f32[384]{0:T(512)}, u32[]{:S(2)}) copy-start(f32[384]{0:T(512)} %get-tuple-element.26) | copy-start | bytes 4612
  269.0 9.2 %collective-permute-start.9 = (bf16[7,1084]{0,1:T(8,128)(2,1)}, bf16[7,1084]{0,1:T(8,128)(2,1)}, u32[]{:S(2)}, u32[]{:S(2)}) collective-permute-start(bf16[7,1084]{0,1:T(8,128)(2,1)} %get-tuple-element.185), channel_id=1, source_target_pairs={{4,0},{8,4},{12,8},{16,12},{20,16},{24,20},{28,24},{5,1},{9,5},{13... | collective-permute-start | bytes 45536 | tf_op jit(solution)/shard_map/ppermute | solution.py:15
  270.3 11.3 %collective-permute-start.8 = (bf16[7,1084]{0,1:T(8,128)(2,1)S(1)}, bf16[7,1084]{0,1:T(8,128)(2,1)}, u32[]{:S(2)}, u32[]{:S(2)}) collective-permute-start(bf16[7,1084]{0,1:T(8,128)(2,1)S(1)} %get-tuple-element.184), channel_id=1, source_target_pairs={{0,4},{4,8},{8,12},{12,16},{16,20},{20,24},{24,28},{1,5},{5,9},{9,... | collective-permute-start | bytes 45536 | tf_op jit(solution)/shard_map/ppermute | solution.py:14
  276.3 9.9 %copy-start.13 = (bf16[384,1024]{0,1:T(8,128)(2,1)S(1)}, bf16[384,1024]{0,1:T(8,128)(2,1)}, u32[]{:S(2)}) copy-start(bf16[384,1024]{0,1:T(8,128)(2,1)} %copy-done.12) | copy-start | bytes 2359300
  277.1 9.0 %copy-start.26 = (bf16[384,15]{0,1:T(8,128)(2,1)}, bf16[384,15]{0,1:T(8,128)(2,1)S(1)}, u32[]{:S(2)}) copy-start(bf16[384,15]{0,1:T(8,128)(2,1)S(1)} %get-tuple-element.270) | copy-start | bytes 34564
  277.1 7.9 %copy-start.28 = (bf16[384,15]{0,1:T(8,128)(2,1)}, bf16[384,15]{0,1:T(8,128)(2,1)S(1)}, u32[]{:S(2)}) copy-start(bf16[384,15]{0,1:T(8,128)(2,1)S(1)} %get-tuple-element.267) | copy-start | bytes 34564
  277.1 7.9 %copy-start.30 = (bf16[384,15]{0,1:T(8,128)(2,1)}, bf16[384,15]{0,1:T(8,128)(2,1)S(1)}, u32[]{:S(2)}) copy-start(bf16[384,15]{0,1:T(8,128)(2,1)S(1)} %get-tuple-element.268) | copy-start | bytes 34564
  277.2 17.0 %collective-permute-start.10 = (bf16[384,60]{0,1:T(8,128)(2,1)S(1)}, bf16[384,60]{0,1:T(8,128)(2,1)S(1)}, u32[]{:S(2)}, u32[]{:S(2)}) collective-permute-start(bf16[384,60]{0,1:T(8,128)(2,1)S(1)} %pad_maximum_fusion.8), channel_id=1, source_target_pairs={{0,1},{1,2},{2,3},{3,0},{4,5},{5,6},{6,7},{7,4},{8,9},{9,10},{10,1... | collective-permute-start | bytes 138248 | tf_op jit(solution)/shard_map/ppermute | solution.py:29
  278.2 15.9 %collective-permute-start.11 = (bf16[384,60]{0,1:T(8,128)(2,1)S(1)}, bf16[384,60]{0,1:T(8,128)(2,1)S(1)}, u32[]{:S(2)}, u32[]{:S(2)}) collective-permute-start(bf16[384,60]{0,1:T(8,128)(2,1)S(1)} %pad_maximum_fusion.8), channel_id=1, source_target_pairs={{0,2},{1,3},{2,0},{3,1},{4,6},{5,7},{6,4},{7,5},{8,10},{9,11},{10,... | collective-permute-start | bytes 138248 | tf_op jit(solution)/shard_map/ppermute | solution.py:29
  281.6 13.8 %collective-permute-start.12 = (bf16[384,60]{0,1:T(8,128)(2,1)S(1)}, bf16[384,60]{0,1:T(8,128)(2,1)S(1)}, u32[]{:S(2)}, u32[]{:S(2)}) collective-permute-start(bf16[384,60]{0,1:T(8,128)(2,1)S(1)} %pad_maximum_fusion.8), channel_id=1, source_target_pairs={{0,3},{1,0},{2,1},{3,2},{4,7},{5,4},{6,5},{7,6},{8,11},{9,8},{10,9... | collective-permute-start | bytes 138248 | tf_op jit(solution)/shard_map/ppermute | solution.py:29
  294.1 7.1 %copy-start.37 = (pred[384]{0:T(512)(128)(4,1)S(1)}, pred[384]{0:T(512)(128)(4,1)}, u32[]{:S(2)}) copy-start(pred[384]{0:T(512)(128)(4,1)} %copy-done.36) | copy-start | bytes 1156
  294.1 7.1 %copy-start.52 = (bf16[1024,60]{0,1:T(8,128)(2,1)S(1)}, bf16[1024,60]{0,1:T(8,128)(2,1)}, u32[]{:S(2)}) copy-start(bf16[1024,60]{0,1:T(8,128)(2,1)} %copy-done.51) | copy-start | bytes 368644
  298.4 8.0 %collective-permute-start.13 = (bf16[60,1024]{1,0:T(8,128)(2,1)S(1)}, bf16[60,1024]{1,0:T(8,128)(2,1)S(1)}, u32[]{:S(2)}, u32[]{:S(2)}) collective-permute-start(bf16[60,1024]{1,0:T(8,128)(2,1)S(1)} %get-tuple-element.194), channel_id=1, source_target_pairs={{0,3},{1,0},{2,1},{3,2},{4,7},{5,4},{6,5},{7,6},{8,11},{9,8},{10,9... | collective-permute-start | bytes 368648 | tf_op jit(solution)/shard_map/ppermute | solution.py:29
  298.5 18.9 %collective-permute-start.14 = (bf16[60,1024]{1,0:T(8,128)(2,1)S(1)}, bf16[60,1024]{1,0:T(8,128)(2,1)S(1)}, u32[]{:S(2)}, u32[]{:S(2)}) collective-permute-start(bf16[60,1024]{1,0:T(8,128)(2,1)S(1)} %get-tuple-element.193), channel_id=1, source_target_pairs={{0,2},{1,3},{2,0},{3,1},{4,6},{5,7},{6,4},{7,5},{8,10},{9,11},{10,... | collective-permute-start | bytes 368648 | tf_op jit(solution)/shard_map/ppermute | solution.py:29
  299.3 18.1 %collective-permute-start.15 = (bf16[60,1024]{1,0:T(8,128)(2,1)S(1)}, bf16[60,1024]{1,0:T(8,128)(2,1)S(1)}, u32[]{:S(2)}, u32[]{:S(2)}) collective-permute-start(bf16[60,1024]{1,0:T(8,128)(2,1)S(1)} %get-tuple-element.192), channel_id=1, source_target_pairs={{0,1},{1,2},{2,3},{3,0},{4,5},{5,6},{6,7},{7,4},{8,9},{9,10},{10,1... | collective-permute-start | bytes 368648 | tf_op jit(solution)/shard_map/ppermute | solution.py:29
  306.5 10.9 %copy-start.23 = (bf16[60,1024]{1,0:T(8,128)(2,1)}, bf16[60,1024]{1,0:T(8,128)(2,1)S(1)}, u32[]{:S(2)}) copy-start(bf16[60,1024]{1,0:T(8,128)(2,1)S(1)} %collective-permute-done.13) | copy-start | bytes 368644
  321.7 6.8 %copy-start.15 = (bf16[340,1024]{1,0:T(8,128)(2,1)}, bf16[340,1024]{1,0:T(8,128)(2,1)S(1)}, u32[]{:S(2)}) copy-start(bf16[340,1024]{1,0:T(8,128)(2,1)S(1)} %concatenate.58) | copy-start | bytes 2088964
  321.7 6.8 %collective-permute-start.16 = (bf16[340,1024]{1,0:T(8,128)(2,1)S(1)}, bf16[340,1024]{1,0:T(8,128)(2,1)S(1)}, u32[]{:S(2)}, u32[]{:S(2)}) collective-permute-start(bf16[340,1024]{1,0:T(8,128)(2,1)S(1)} %concatenate.58), channel_id=1, source_target_pairs={{0,4},{4,0},{8,12},{12,8},{16,20},{20,16},{24,28},{28,24},{1,5},{5... | collective-permute-start | bytes 2088968 | tf_op jit(solution)/shard_map/ppermute | solution.py:34
  321.8 12.0 %copy-start.4 = (bf16[2,2,1,256,2048]{4,3,2,1,0:T(8,128)(2,1)S(1)}, bf16[2,2,1,256,2048]{4,3,2,1,0:T(8,128)(2,1)}, u32[]{:S(2)}) copy-start(bf16[2,2,1,256,2048]{4,3,2,1,0:T(8,128)(2,1)} %get-tuple-element.158) | copy-start | bytes 12582916
  329.9 6.4 %copy-start.14 = (bf16[340,1024]{1,0:T(8,128)(2,1)}, bf16[340,1024]{1,0:T(8,128)(2,1)S(1)}, u32[]{:S(2)}) copy-start(bf16[340,1024]{1,0:T(8,128)(2,1)S(1)} %add_convert_fusion.8) | copy-start | bytes 2088964
  330.8 21.1 %collective-permute-start.17 = (bf16[180,1024]{1,0:T(8,128)(2,1)S(1)}, bf16[180,1024]{1,0:T(8,128)(2,1)}, u32[]{:S(2)}, u32[]{:S(2)}) collective-permute-start(bf16[180,1024]{1,0:T(8,128)(2,1)S(1)} %slice.812), channel_id=1, source_target_pairs={{0,16},{4,20},{8,24},{12,28},{16,0},{20,4},{24,8},{28,12},{1,17},{... | collective-permute-start | bytes 1105928 | tf_op jit(solution)/shard_map/ppermute | solution.py:34
  332.3 17.3 %collective-permute-start.19 = (bf16[160,1024]{1,0:T(8,128)(2,1)}, bf16[160,1024]{1,0:T(8,128)(2,1)}, u32[]{:S(2)}, u32[]{:S(2)}) collective-permute-start(bf16[160,1024]{1,0:T(8,128)(2,1)} %slice.814), channel_id=1, source_target_pairs={{0,8},{4,12},{8,0},{12,4},{16,24},{20,28},{24,16},{28,20},{1,9},{5... | collective-permute-start | bytes 983048 | tf_op jit(solution)/shard_map/ppermute | solution.py:34
  351.6 10.0 %collective-permute-start.20 = (bf16[160,1024]{1,0:T(8,128)(2,1)}, bf16[160,1024]{1,0:T(8,128)(2,1)}, u32[]{:S(2)}, u32[]{:S(2)}) collective-permute-start(bf16[160,1024]{1,0:T(8,128)(2,1)} %add_convert_fusion.12), channel_id=1, source_target_pairs={{0,16},{4,20},{8,24},{12,28},{16,0},{20,4},{24,8},{28,12},{1,17},{... | collective-permute-start | bytes 983048 | tf_op jit(solution)/shard_map/ppermute | solution.py:34
  353.2 8.3 %copy-start.17 = (bf16[180,1024]{1,0:T(8,128)(2,1)}, bf16[180,1024]{1,0:T(8,128)(2,1)S(1)}, u32[]{:S(2)}) copy-start(bf16[180,1024]{1,0:T(8,128)(2,1)S(1)} %add_convert_fusion.10) | copy-start | bytes 1105924
  353.2 10.3 %collective-permute-start.18 = (bf16[180,1024]{1,0:T(8,128)(2,1)S(1)}, bf16[180,1024]{1,0:T(8,128)(2,1)}, u32[]{:S(2)}, u32[]{:S(2)}) collective-permute-start(bf16[180,1024]{1,0:T(8,128)(2,1)S(1)} %add_convert_fusion.10), channel_id=1, source_target_pairs={{0,8},{4,12},{8,0},{12,4},{16,24},{20,28},{24,16},{28,20},{1,9},{5... | collective-permute-start | bytes 1105928 | tf_op jit(solution)/shard_map/ppermute | solution.py:34
  378.4 48.9 %collective-permute-start.24 = (bf16[2,256,2048]{2,1,0:T(8,128)(2,1)}, bf16[2,256,2048]{2,1,0:T(8,128)(2,1)}, u32[]{:S(2)}, u32[]{:S(2)}) collective-permute-start(bf16[2,256,2048]{2,1,0:T(8,128)(2,1)} %get-tuple-element.169), channel_id=1, source_target_pairs={{0,8},{4,12},{8,0},{12,4},{16,24},{20,28},{24,16},{28,20},{1,9},{5... | collective-permute-start | bytes 6291464 | tf_op jit(solution)/shard_map/ppermute | solution.py:34
  383.4 48.9 %collective-permute-start.22 = (bf16[2,256,2048]{2,1,0:T(8,128)(2,1)}, bf16[2,256,2048]{2,1,0:T(8,128)(2,1)}, u32[]{:S(2)}, u32[]{:S(2)}) collective-permute-start(bf16[2,256,2048]{2,1,0:T(8,128)(2,1)} %get-tuple-element.163), channel_id=1, source_target_pairs={{0,16},{4,20},{8,24},{12,28},{16,0},{20,4},{24,8},{28,12},{1,17},{... | collective-permute-start | bytes 6291464 | tf_op jit(solution)/shard_map/ppermute | solution.py:34
  396.8 5.7 %copy-start.6 = (bf16[2,2,1,256,2048]{4,3,2,1,0:T(8,128)(2,1)S(1)}, bf16[2,2,1,256,2048]{4,3,2,1,0:T(8,128)(2,1)}, u32[]{:S(2)}) copy-start(bf16[2,2,1,256,2048]{4,3,2,1,0:T(8,128)(2,1)} %get-tuple-element.160) | copy-start | bytes 12582916
  401.1 71.1 %collective-permute-start.29 = (bf16[2,256,2048]{1,2,0:T(8,128)(2,1)}, bf16[2,256,2048]{1,2,0:T(8,128)(2,1)}, u32[]{:S(2)}, u32[]{:S(2)}) collective-permute-start(bf16[2,256,2048]{1,2,0:T(8,128)(2,1)} %fusion.12), channel_id=1, source_target_pairs={{0,8},{4,12},{8,0},{12,4},{16,24},{20,28},{24,16},{28,20},{1,9},{5... | collective-permute-start | bytes 6291464 | tf_op jit(solution)/shard_map/ppermute | solution.py:34
  413.1 64.1 %collective-permute-start.27 = (bf16[2,256,2048]{1,2,0:T(8,128)(2,1)}, bf16[2,256,2048]{1,2,0:T(8,128)(2,1)}, u32[]{:S(2)}, u32[]{:S(2)}) collective-permute-start(bf16[2,256,2048]{1,2,0:T(8,128)(2,1)} %fusion.11), channel_id=1, source_target_pairs={{0,16},{4,20},{8,24},{12,28},{16,0},{20,4},{24,8},{28,12},{1,17},{... | collective-permute-start | bytes 6291464 | tf_op jit(solution)/shard_map/ppermute | solution.py:34
  422.2 5.1 copy-start.8
  425.1 7.2 %copy-start.9 = (bf16[1,2,1,256,2048]{4,3,2,1,0:T(8,128)(2,1)S(1)}, bf16[1,2,1,256,2048]{4,3,2,1,0:T(8,128)(2,1)}, u32[]{:S(2)}) copy-start(bf16[1,2,1,256,2048]{4,3,2,1,0:T(8,128)(2,1)} %get-tuple-element.162) | copy-start | bytes 6291460
  428.9 6.4 %copy-start.7 = (bf16[1,2,1,256,2048]{3,4,2,1,0:T(8,128)(2,1)S(1)}, bf16[1,2,1,256,2048]{3,4,2,1,0:T(8,128)(2,1)}, u32[]{:S(2)}) copy-start(bf16[1,2,1,256,2048]{3,4,2,1,0:T(8,128)(2,1)} %copy.246) | copy-start | bytes 6291460
  428.9 70.7 %collective-permute-start.25 = (bf16[256,2048]{1,0:T(8,128)(2,1)S(1)}, bf16[256,2048]{1,0:T(8,128)(2,1)S(1)}, u32[]{:S(2)}, u32[]{:S(2)}) collective-permute-start(bf16[256,2048]{1,0:T(8,128)(2,1)S(1)} %fusion.29), channel_id=1, source_target_pairs={{0,16},{4,20},{8,24},{12,28},{16,0},{20,4},{24,8},{28,12},{1,17},{... | collective-permute-start | bytes 3145736 | tf_op jit(solution)/shard_map/ppermute | solution.py:34
  433.9 67.4 %collective-permute-start.23 = (bf16[256,2048]{1,0:T(8,128)(2,1)S(1)}, bf16[256,2048]{1,0:T(8,128)(2,1)S(1)}, u32[]{:S(2)}, u32[]{:S(2)}) collective-permute-start(bf16[256,2048]{1,0:T(8,128)(2,1)S(1)} %fusion.27), channel_id=1, source_target_pairs={{0,8},{4,12},{8,0},{12,4},{16,24},{20,28},{24,16},{28,20},{1,9},{5... | collective-permute-start | bytes 3145736 | tf_op jit(solution)/shard_map/ppermute | solution.py:34
  473.7 46.1 %collective-permute-start.30 = (bf16[256,2048]{0,1:T(8,128)(2,1)S(1)}, bf16[256,2048]{0,1:T(8,128)(2,1)S(1)}, u32[]{:S(2)}, u32[]{:S(2)}) collective-permute-start(bf16[256,2048]{0,1:T(8,128)(2,1)S(1)} %fusion.33), channel_id=1, source_target_pairs={{0,16},{4,20},{8,24},{12,28},{16,0},{20,4},{24,8},{28,12},{1,17},{... | collective-permute-start | bytes 3145736 | tf_op jit(solution)/shard_map/ppermute | solution.py:34
  478.7 42.6 %collective-permute-start.28 = (bf16[256,2048]{0,1:T(8,128)(2,1)S(1)}, bf16[256,2048]{0,1:T(8,128)(2,1)S(1)}, u32[]{:S(2)}, u32[]{:S(2)}) collective-permute-start(bf16[256,2048]{0,1:T(8,128)(2,1)S(1)} %fusion.31), channel_id=1, source_target_pairs={{0,8},{4,12},{8,0},{12,4},{16,24},{20,28},{24,16},{28,20},{1,9},{5... | collective-permute-start | bytes 3145736 | tf_op jit(solution)/shard_map/ppermute | solution.py:34
  (32 other events, 93.8 us)
Sparse Core Ops, SparseCore 0:
  10.2 75.6 all-gather.2
  87.4 64.5 all-gather.4
  181.3 58.8 reduce-scatter.4
  242.4 66.7 reduce-scatter.2

commit v2 on v1

--- a/solution.py
+++ b/solution.py
@@ -38,51 +38,48 @@
     return (lax.axis_index("seq") // (1 << bit)) % 2
 
 
-def scatter_sum(pieces, bits, order):
-    bits = list(bits)
-    for bit in order:
-        axis = bits.index(bit)
-        bits.pop(axis)
-        mine = my_bit(bit)
-
-        def part(which):
-            total = 0.0
-            for piece in pieces:
-                total = total + lax.dynamic_index_in_dim(
-                    piece, which, axis, keepdims=False
-                ).astype(jnp.float32)
-            return total.astype(jnp.bfloat16)
-
-        pieces = [part(mine), swapped(part(1 - mine), bit)]
-    return pieces[0].astype(jnp.float32) + pieces[1].astype(jnp.float32)
-
-
 def seq_bits():
     return lax.axis_size("seq").bit_length() - 1
 
 
-def weight_grad(features, factor):
+def chosen(pieces, which, axis):
+    total = 0.0
+    for piece in pieces:
+        part = lax.dynamic_index_in_dim(piece, which, axis, keepdims=False)
+        total = total + part.astype(jnp.float32)
+    return total.astype(jnp.bfloat16)
+
+
+def first_halves(features, factor):
     count, depth = seq_bits(), features.shape[0]
     rows = features.shape[1] >> count
     grouped = features.reshape(depth, 1 << (count - 1), 2, rows)
-    width = factor.shape[1]
-
-    def half(which, factor):
-        chosen = lax.dynamic_index_in_dim(grouped, which, 2, keepdims=False)
-        return dot(chosen.reshape(depth, -1), factor, ((0,), (0,))).astype(jnp.bfloat16)
-
+    width = factor.shape[1] // 2
+    shape = (2,) * (count - 1) + (rows, width)
     mine = my_bit(0)
-    sent = half(1 - mine, factor)
-    sent, factor = lax.optimization_barrier((sent, factor))
-    got = swapped(sent, 0)
-    kept = half(mine, factor)
-    shape = (2,) * (count - 1) + (2, rows // 2, width)
-    bits = list(range(count - 1, 0, -1))
-    pieces = [kept.reshape(shape), got.reshape(shape)]
-    lead = len(bits)
-    upper = scatter_sum([lax.index_in_dim(p, 0, lead, False) for p in pieces], bits, bits)
-    lower = scatter_sum([lax.index_in_dim(p, 1, lead, False) for p in pieces], bits, bits[::-1])
-    return jnp.concatenate([upper, lower], axis=0)
+    other = lax.dynamic_index_in_dim(grouped, 1 - mine, 2, keepdims=False).reshape(depth, -1)
+    own = lax.dynamic_index_in_dim(grouped, mine, 2, keepdims=False).reshape(depth, -1)
+    sent = []
+    for side in range(2):
+        columns = factor[:, side * width : (side + 1) * width]
+        sent.append(dot(other, columns, ((0,), (0,))).astype(jnp.bfloat16).reshape(shape))
+
+    def kept(factor):
+        result = []
+        for side in range(2):
+            columns = factor[:, side * width : (side + 1) * width]
+            result.append(dot(own, columns, ((0,), (0,))).astype(jnp.bfloat16).reshape(shape))
+        return result
+
+    return sent, kept
+
+
+def send_parts(pieces, bits, bit):
+    return chosen(pieces, 1 - my_bit(bit), bits.index(bit))
+
+
+def keep_parts(pieces, bits, bit):
+    return chosen(pieces, my_bit(bit), bits.index(bit))
 
 
 def seq_sum(values):
@@ -162,32 +159,67 @@
     back_part = dot(up_weight, pre_grad, ((1,), (1,))).astype(bf16)
     back_part, middle, pre_grad = lax.optimization_barrier((back_part, middle, pre_grad))
     act_back = lax.psum_scatter(back_part, "tp", scatter_dimension=0, tiled=True)
-    down_grad = weight_grad(full_cot, middle).T
-    up_grad = weight_grad(full_act, pre_grad)
+    down_sent, down_kept = first_halves(full_cot, middle)
+    up_sent, up_kept = first_halves(full_act, pre_grad)
+    down_sent, up_sent, middle, pre_grad = lax.optimization_barrier(
+        (down_sent, up_sent, middle, pre_grad)
+    )
+    got = [swapped(block, 0) for block in down_sent + up_sent]
+    kept = down_kept(middle) + up_kept(pre_grad)
+    kept, middle = lax.optimization_barrier((kept, middle))
     ffn_part = dot(down_weight, middle, ((0,), (1,))).astype(bf16)
     ffn_total = lax.psum_scatter(ffn_part, "tp", scatter_dimension=0, tiled=True)
+    high_bits = list(range(seq_bits() - 1, 0, -1))
+    orders = [high_bits, high_bits[::-1]] * 2
+    lines = [[one, two] for one, two in zip(kept, got)]
+    left = [list(high_bits) for _ in lines]
+
+    def send_all(which, step):
+        return [send_parts(lines[i], left[i], orders[i][step]) for i in which]
+
+    def swap_all(which, step, sent):
+        return [swapped(block, orders[i][step]) for i, block in zip(which, sent)]
+
+    def join_all(which, step, got):
+        for i, block in zip(which, got):
+            lines[i] = [keep_parts(lines[i], left[i], orders[i][step]), block]
+            left[i].remove(orders[i][step])
+
+    downs, ups = (0, 1), (2, 3)
+    down_sent, up_sent = send_all(downs, 0), send_all(ups, 0)
+    act_back, down_sent, up_sent = lax.optimization_barrier((act_back, down_sent, up_sent))
+    down_got, up_got = swap_all(downs, 0, down_sent), swap_all(ups, 0, up_sent)
     layer_output = (act.astype(f32) + ffn_total.astype(f32).T).astype(bf16)
 
     act_grad = cotangent.astype(f32) + act_back.astype(f32).T
     short_grad = act_grad.astype(bf16)
     kernel_short = jnp.concatenate(kernels, axis=1).astype(bf16)
-    joined = jnp.concatenate([short_grad, kernel_short], axis=1)
-    low, high = halo(joined[:reach], joined[tok_rows - reach :])
+    low, high = halo(
+        jnp.concatenate([short_grad[:reach], kernel_short[:reach]], axis=1),
+        jnp.concatenate([short_grad[tok_rows - reach :], kernel_short[tok_rows - reach :]], axis=1),
+    )
     grad_pad = jnp.concatenate([low[:, :feat_width], short_grad, high[:, :feat_width]], axis=0)
     kernel_pad = jnp.concatenate([low[:, feat_width:], kernel_short, high[:, feat_width:]], axis=0)
-    logit_grads = []
+    taps_at = jnp.arange(gen_cols)
+    kernel_grad = jnp.zeros((tok_rows, gen_cols), f32)
     for head in range(head_count):
         columns = slice(head * head_width, (head + 1) * head_width)
         scores = dot(short_grad[:, columns], padded[:, columns], ((1,), (1,)))
-        kernel_grad = jnp.stack(
-            [jnp.sum(jnp.where(ahead == tap, scores, 0.0), axis=-1) for tap in range(KW)], axis=-1
-        )
-        weighted = jnp.sum(kernels[head] * kernel_grad, axis=-1, keepdims=True)
-        logit_grads.append((kernels[head] * (kernel_grad - weighted)).astype(bf16))
-    logit_grad = jnp.concatenate(logit_grads, axis=1)
+        for tap in range(KW):
+            one = jnp.sum(jnp.where(ahead == tap, scores, 0.0), axis=-1, keepdims=True)
+            kernel_grad = jnp.where(taps_at[None, :] == head * KW + tap, one, kernel_grad)
+    kernel = jnp.concatenate(kernels, axis=1)
+    same_head = (taps_at[:, None] // KW == taps_at[None, :] // KW).astype(f32)
+    weighted = jnp.dot(kernel * kernel_grad, same_head, precision=lax.Precision.HIGHEST)
+    logit_grad = (kernel * (kernel_grad - weighted)).astype(bf16)
+    logit_grad, down_got = lax.optimization_barrier((logit_grad, down_got))
+    join_all(downs, 0, down_got)
+    down_sent = send_all(downs, 1)
     logit_grads = jnp.concatenate(
         [logit_grad] + [turned(logit_grad, shift) for shift in range(1, tp_count)], axis=1
     )
+
+    logit_grads, up_got = lax.optimization_barrier((logit_grads, up_got))
 
     behind = jnp.arange(tok_rows)[None, :] - jnp.arange(long_rows)[:, None] + 2 * reach
     conv_back = []
@@ -209,7 +241,20 @@
     table_part = dot(
         onehot.astype(bf16), jnp.where(masked, hidden_grad, f32(0.0)).astype(bf16), ((0,), (0,))
     ).astype(bf16)
-    summed = seq_sum(jnp.concatenate(gen_owned + [table_part], axis=0))
+    sums = jnp.concatenate(gen_owned + [table_part], axis=0)
+    join_all(ups, 0, up_got)
+    up_sent = send_all(ups, 1)
+    down_got = swap_all(downs, 1, down_sent)
+    sums, up_sent, down_got = lax.optimization_barrier((sums, up_sent, down_got))
+    up_got = swap_all(ups, 1, up_sent)
+    join_all(downs, 1, down_got)
+    join_all(ups, 1, up_got)
+    for step in range(2, len(high_bits)):
+        join_all(range(4), step, swap_all(range(4), step, send_all(range(4), step)))
+    ends = [one.astype(f32) + two.astype(f32) for one, two in lines]
+    down_grad = jnp.concatenate(ends[:2], axis=1).T
+    up_grad = jnp.concatenate(ends[2:], axis=1)
+    summed = seq_sum(sums)
     gen_total = tp_count * gen_cols
     table_grad = summed[gen_total:].astype(f32)
     gen_sum = summed[:gen_total].reshape(tp_count, gen_cols, feat_width)

time: 539 us -> 517 us (0.959)
  local copies, waits for them, and re-layouts: 113 us -> 80.4 us
  matrix products: 99.1 us -> 110 us
  starting transfers between devices: 49.5 us -> 40.8 us
    ppermute x12, waiting for transfers between devices: 30.4 us -> 57 us  [turned(): lax.ppermute(block, 'tp', [(i, (i + shift) % count) for i in range(count)])]
    optimization_barrier x0 -> x4, local copies, waits for them, and re-layouts: none -> 24.9 us  [the longest x2 12.5 us: body(): kept, middle = lax.optimization_barrier((kept, middle))]
    all_gather x1, waiting for transfers between devices: 31.4 us -> 6.54 us  [body(): full_cot = lax.all_gather(cotangent, 'tp', axis=1, tiled=True)]
    unnamed x136 -> x145, local copies, waits for them, and re-layouts: 43.5 us -> 20.4 us
    slice x5 -> x2, local copies, waits for them, and re-layouts: 21 us -> 0.02 us  [the longest x1 0.01 us: body(): short_grad[tok_rows - reach:]]
    another operation x64 -> x0, local copies, waits for them, and re-layouts: 14.3 us -> none  [body(): jnp.stack([jnp.sum(jnp.where(ahead == tap, scores, 0.0), axis=-1) for tap...]
    ppermute x15 -> x17, waiting for transfers between devices: 76.8 us -> 89.9 us  [swapped(): return lax.ppermute(block, 'seq', [(i, i ^ 1 << bit) for i in range(count)])]
    concatenate x3 -> x1, local copies, waits for them, and re-layouts: 14.4 us -> 5.14 us  [body(): sums = jnp.concatenate(gen_owned + [table_part], axis=0)]
  transfers between devices with their start and end apart: 35 -> 37, of which waited for: 14 -> 18; matrix products, arithmetic and copies ran while one was open for 43% -> 42% of each run, Pallas kernels for 0% -> 0%
where the time goes in v2:
time: 517 us; the launch traced here: 508 us
  waiting for transfers between devices  201 us (39%)
  matrix products  110 us (21%)
  local copies, waits for them, and re-layouts  80.4 us (16%)
  other arithmetic  59.8 us (12%)
  starting transfers between devices  40.8 us (8%)
  between operations  15.6 us (3%)
    dot_general x29, matrix products, dot(): lax.dot_general(a, b, (dims, ((), ())), preferred_element_type=jnp.float32)  103 us
    ppermute x17, waiting for transfers between devices, swapped(): return lax.ppermute(block, 'seq', [(i, i ^ 1 << bit) for i in range(count)])  89.9 us
    ppermute x12, waiting for transfers between devices, turned(): lax.ppermute(block, 'tp', [(i, (i + shift) % count) for i in range(count)])  57 us
    all_gather x1, waiting for transfers between devices, body(): full_act = lax.all_gather(act, 'tp', axis=1, tiled=True)  47.8 us
    convert_element_type x8, other arithmetic, chosen(): return total.astype(jnp.bfloat16)  30.3 us
    unnamed x145, local copies, waits for them, and re-layouts  20.4 us
    ppermute x12, starting transfers between devices, turned(): lax.ppermute(block, 'tp', [(i, (i + shift) % count) for i in range(count)])  19.7 us
    ppermute x17, starting transfers between devices, swapped(): return lax.ppermute(block, 'seq', [(i, i ^ 1 << bit) for i in range(count)])  13.1 us
  transfers between devices with their start and end apart: 37, of which 18 were waited for; matrix products, arithmetic and copies ran while one was open for 42% of the time, Pallas kernels for 0%

profile of v2, /device:TPU:0, one launch (start us, length us, event | category | flops | bytes accessed | tf_op | source)
XLA Modules:
  0.0 508.0 jit_solution(17102755452381265741)
XLA Ops:
  7.3 2.4 copy.63
  9.9 3.1 collective-permute-start
  12.9 2.1 collective-permute-start.2
  20.7 12.4 %collective-permute-done.1 = bf16[1024,60]{0,1:T(8,128)(2,1)S(1)} collective-permute-done((bf16[1024,60]{0,1:T(8,128)(2,1)S(1)}, bf16[1024,60]{0,1:T(8,128)(2,1)S(1)}, u32[]{:S(2)}, u32[]{:S(2)}) %collective-permute-start.1) | collective-permute-done | bytes 122912 | tf_op jit(solution)/shard_map/ppermute | solution.py:29
  33.8 5.2 %collective-permute-start.3 = (f32[384,60]{1,0:T(8,128)S(1)}, f32[384,60]{1,0:T(8,128)S(1)}, u32[]{:S(2)}, u32[]{:S(2)}) collective-permute-start(f32[384,60]{1,0:T(8,128)S(1)} %get-tuple-element.278), channel_id=1, source_target_pairs={{0,3},{1,0},{2,1},{3,2},{4,7},{5,4},{6,5},{7,6},{8,11},{9,8},{10,9... | collective-permute-start | bytes 276488 | tf_op jit(solution)/shard_map/ppermute | solution.py:29
  39.9 9.7 %collective-permute-done.3 = f32[384,60]{1,0:T(8,128)S(1)} collective-permute-done((f32[384,60]{1,0:T(8,128)S(1)}, f32[384,60]{1,0:T(8,128)S(1)}, u32[]{:S(2)}, u32[]{:S(2)}) %collective-permute-start.3) | collective-permute-done | bytes 92192 | tf_op jit(solution)/shard_map/ppermute | solution.py:29
  49.7 26.1 %collective-permute-done.4 = f32[384,60]{1,0:T(8,128)S(1)} collective-permute-done((f32[384,60]{1,0:T(8,128)S(1)}, f32[384,60]{1,0:T(8,128)S(1)}, u32[]{:S(2)}, u32[]{:S(2)}) %collective-permute-start.4) | collective-permute-done | bytes 92192 | tf_op jit(solution)/shard_map/ppermute | solution.py:29
  76.7 1.6 slice_reduce_fusion.59
  78.3 1.6 slice_reduce_fusion.14
  79.9 1.6 slice_reduce_fusion.44
  81.5 1.6 slice_reduce_fusion.29
  88.4 6.5 %all-gather.3.cloned.1.call-done = bf16[384,4096]{0,1:T(8,128)(2,1)} async-done(((bf16[384,1024]{0,1:T(8,128)(2,1)}), bf16[384,4096]{0,1:T(8,128)(2,1)}) %all-gather.3.cloned.1.call-update) | async-done | bytes 3145744 | tf_op jit(solution)/shard_map/all_gather | solution.py:151
  94.9 4.0 constant_dynamic-slice_fusion.2
  98.9 12.4 %fusion.558 = f32[384,2048]{1,0:T(8,128)} fusion(bf16[384,4096]{0,1:T(8,128)(2,1)S(1)} %copy-done.15, bf16[2048,4096]{1,0:T(8,128)(2,1)} %param.14), kind=kOutput, calls=%fused_computation.895 | convolution fusion | flops 6442450944 | bytes 23068672 | tf_op jit(solution)/shard_map/dot_general | solution.py:24
  111.3 47.8 %all-gather.5.cloned.1.call-done = bf16[384,4096]{1,0:T(8,128)(2,1)} async-done(((bf16[384,1024]{1,0:T(8,128)(2,1)}), bf16[384,4096]{1,0:T(8,128)(2,1)}) %all-gather.5.cloned.1.call-update) | async-done | bytes 3145744 | tf_op jit(solution)/shard_map/all_gather | solution.py:152
  159.1 16.6 %multiply_convert_fusion = (bf16[384,2048]{1,0:T(8,128)(2,1)}, bf16[384,2048]{1,0:T(8,128)(2,1)S(1)}) fusion(f32[384,2048]{1,0:T(8,128)} %fusion.558, bf16[384,4096]{1,0:T(8,128)(2,1)} %all-gather.5.cloned.1.call-done, bf16[4096,2048]{1,0:T(8,128)(2,1)} %param.13), kind=kOutput, calls=%fused_computation.31 | convolution fusion | flops 6459752448 | bytes 26214400 | tf_op jit(solution)/shard_map/dot_general | solution.py:24
  175.7 12.0 %fusion = bf16[4096,384]{0,1:T(8,128)(2,1)} fusion(bf16[384,2048]{1,0:T(8,128)(2,1)S(1)} %get-tuple-element.39, bf16[4096,2048]{1,0:T(8,128)(2,1)} %param.13), kind=kOutput, calls=%fused_computation.2 | convolution fusion | flops 6444023808 | bytes 21495808 | tf_op jit(solution)/shard_map/dot_general | solution.py:24
  188.2 6.3 %reshape.578 = bf16[384,4,2,512]{3,2,1,0:T(2,128)(2,1)} reshape(bf16[384,4096]{1,0:T(8,128)(2,1)} %all-gather.5.cloned.1.call-done) | data formatting | bytes 6291456 | tf_op jit(solution)/shard_map/reshape | solution.py:56
  194.5 12.0 %constant_dynamic-slice_fusion = (bf16[384,4,1,512]{3,2,1,0:T(2,128)(2,1)}, bf16[384,4,1,512]{3,2,1,0:T(2,128)(2,1)}) fusion(bf16[384,4,2,512]{3,2,1,0:T(2,128)(2,1)} %reshape.578, s32[]{:T(128)S(6)} %select_n.979, s32[]{:T(128)S(6)} %select_n.980), kind=kLoop, calls=%fused_computation.691 | loop fusion | bytes 6291464 | tf_op jit(solution)/shard_map/jit(dynamic_index_in_dim)/dynamic_slice | solution.py:61
  206.5 7.1 %copy.88 = bf16[384,4,1,512]{0,3,1,2:T(8,128)(2,1)S(1)} copy(bf16[384,4,1,512]{3,2,1,0:T(2,128)(2,1)} %get-tuple-element.261) | data formatting | bytes 3145728
  213.6 5.6 %convolution_convert_fusion.6 = bf16[2048,1024]{1,0:T(8,128)(2,1)} fusion(bf16[384,2048]{0,1:T(8,128)(2,1)S(1)} %bitcast.130, bf16[384,2048]{1,0:T(8,128)(2,1)} %copy-done.67), kind=kOutput, calls=%fused_computation.20 | convolution fusion | flops 1612709888 | bytes 6553600 | tf_op jit(solution)/shard_map/dot_general | solution.py:24
  219.3 4.3 convolution_convert_fusion.7
  223.5 4.4 convolution_convert_fusion.8
  227.9 4.3 convolution_convert_fusion.9
  232.2 6.2 %copy.67 = bf16[2,2,512,1024]{2,3,1,0:T(8,128)(2,1)} copy(bf16[2,2,512,1024]{3,2,1,0:T(8,128)(2,1)} %bitcast.123) | data formatting | bytes 8388608 | tf_op jit(solution)/shard_map/optimization_barrier | solution.py:164
  240.7 6.2 %copy.69 = bf16[2,2,512,1024]{2,3,1,0:T(8,128)(2,1)} copy(bf16[2,2,512,1024]{3,2,1,0:T(8,128)(2,1)} %bitcast.121) | data formatting | bytes 8388608 | tf_op jit(solution)/shard_map/optimization_barrier | solution.py:164
  249.3 7.2 %copy.89 = bf16[384,4,1,512]{0,3,1,2:T(8,128)(2,1)S(1)} copy(bf16[384,4,1,512]{3,2,1,0:T(2,128)(2,1)} %get-tuple-element.260) | data formatting | bytes 3145728
  256.5 5.6 %convolution_convert_fusion.2 = bf16[2048,1024]{1,0:T(8,128)(2,1)} fusion(bf16[384,2048]{0,1:T(8,128)(2,1)S(1)} %bitcast.128, bf16[384,2048]{1,0:T(8,128)(2,1)} %copy-done.67), kind=kOutput, calls=%fused_computation.16 | convolution fusion | flops 1612709888 | bytes 6553600 | tf_op jit(solution)/shard_map/dot_general | solution.py:24
  262.1 4.3 convolution_convert_fusion.3
  266.4 4.3 convolution_convert_fusion.4
  270.7 4.4 convolution_convert_fusion.5
  275.1 6.2 %copy.66 = bf16[2,2,512,1024]{2,3,1,0:T(8,128)(2,1)} copy(bf16[2,2,512,1024]{3,2,1,0:T(8,128)(2,1)} %bitcast.124) | data formatting | bytes 8388608 | tf_op jit(solution)/shard_map/optimization_barrier | solution.py:169
  281.3 6.3 %copy.68 = bf16[2,2,512,1024]{2,3,1,0:T(8,128)(2,1)} copy(bf16[2,2,512,1024]{3,2,1,0:T(8,128)(2,1)} %bitcast.122) | data formatting | bytes 8388608 | tf_op jit(solution)/shard_map/optimization_barrier | solution.py:169
  287.6 11.7 %fusion.1 = bf16[4096,384]{0,1:T(8,128)(2,1)} fusion(bf16[384,2048]{1,0:T(8,128)(2,1)S(1)} %copy-done.66, bf16[2048,4096]{1,0:T(8,128)(2,1)} %param.14), kind=kOutput, calls=%fused_computation.3 | convolution fusion | flops 6444023808 | bytes 21495808 | tf_op jit(solution)/shard_map/dot_general | solution.py:24
  299.4 6.9 %add_convert_fusion.1 = (bf16[1,2,512,1024]{2,3,1,0:T(8,128)(2,1)}, bf16[2,512,1024]{1,2,0:T(8,128)(2,1)}) fusion(bf16[2,2,512,1024]{2,3,1,0:T(8,128)(2,1)} %collective-permute-done.8, s32[]{:T(128)S(6)} %select_n.1170, bf16[2,2,512,1024]{2,3,1,0:T(8,128)(2,1)} %copy.66, s32[]{:T(128)S(6)} %select_n.983), kind=kLoop, calls=%fused_computation.9 | loop fusion | flops 8388608 | bytes 12582920 | tf_op jit(solution)/shard_map/convert_element_type | solution.py:50
  306.3 5.9 %add_convert_fusion.3 = (bf16[1,2,512,1024]{3,2,1,0:T(8,128)(2,1)S(1)}, bf16[2,512,1024]{2,1,0:T(8,128)(2,1)}) fusion(bf16[2,2,512,1024]{3,2,1,0:T(8,128)(2,1)} %collective-permute-done.10, s32[]{:T(128)S(6)} %select_n.1170, bf16[2,2,512,1024]{3,2,1,0:T(8,128)(2,1)S(1)} %bitcast.120, s32[]{:T(128)S(6)} %select_n.983), kind=kLoop, calls=%fused_computation.11 | loop fusion | flops 8388608 | bytes 12582920 | tf_op jit(solution)/shard_map/convert_element_type | solution.py:50
  312.3 5.7 %add_convert_fusion = (bf16[2,1,512,1024]{2,3,1,0:T(8,128)(2,1)}, bf16[2,512,1024]{1,2,0:T(8,128)(2,1)}) fusion(bf16[2,2,512,1024]{2,3,1,0:T(8,128)(2,1)} %collective-permute-done.9, s32[]{:T(128)S(6)} %select_n.1171, bf16[2,2,512,1024]{2,3,1,0:T(8,128)(2,1)S(1)} %copy-done.2, s32[]{:T(128)S(6)} %select_n.986), kind=kLoop, calls=%fused_computation.8 | loop fusion | flops 8388608 | bytes 12582920 | tf_op jit(solution)/shard_map/convert_element_type | solution.py:50
  317.9 6.5 %add_convert_fusion.2 = (bf16[2,1,512,1024]{3,2,1,0:T(8,128)(2,1)}, bf16[2,512,1024]{2,1,0:T(8,128)(2,1)}) fusion(bf16[2,2,512,1024]{3,2,1,0:T(8,128)(2,1)} %collective-permute-done.11, s32[]{:T(128)S(6)} %select_n.1171, bf16[2,2,512,1024]{3,2,1,0:T(8,128)(2,1)S(1)} %bitcast.119, s32[]{:T(128)S(6)} %select_n.986), kind=kLoop, calls=%fused_computation.10 | loop fusion | flops 8388608 | bytes 12582920 | tf_op jit(solution)/shard_map/convert_element_type | solution.py:50
  324.4 1.6 fusion.24
  327.4 3.3 collective-permute-start.12
  330.7 2.1 collective-permute-start.14
  337.8 6.6 %fusion.27 = bf16[384,60]{1,0:T(8,128)(2,1)S(1)} fusion(f32[384,60]{1,0:T(8,128)S(1)} %get-tuple-element.251, f32[384]{0:T(512)S(1)} %get-tuple-element.112, f32[384]{0:T(512)S(1)} %get-tuple-element.113, f32[384]{0:T(512)S(1)} %get-tuple-element.114, f32[384]{0:T(512)S(1)} %get-tuple-element.115, f32[384]{0:T(512)S(1)} %get-tuple-element.116, ...), kind=kOutput, calls=%fused_computation.72 | convolution fusion | flops 19449360 | bytes 234240 | tf_op jit(solution)/shard_map/dot_general | solution.py:213
  355.3 24.0 %collective-permute-done.14 = bf16[2,512,1024]{1,2,0:T(8,128)(2,1)S(1)} collective-permute-done((bf16[2,512,1024]{1,2,0:T(8,128)(2,1)}, bf16[2,512,1024]{1,2,0:T(8,128)(2,1)S(1)}, u32[]{:S(2)}, u32[]{:S(2)}) %collective-permute-start.14) | collective-permute-done | bytes 2097184 | tf_op jit(solution)/shard_map/ppermute | solution.py:34
  379.2 2.2 collective-permute-done.15
  381.4 1.9 collective-permute-start.18
  387.6 4.3 collective-permute-done.17
  393.6 30.5 %collective-permute-done.19 = bf16[2,512,1024]{2,1,0:T(8,128)(2,1)S(1)} collective-permute-done((bf16[2,512,1024]{2,1,0:T(8,128)(2,1)S(1)}, bf16[2,512,1024]{2,1,0:T(8,128)(2,1)S(1)}, u32[]{:S(2)}, u32[]{:S(2)}) %collective-permute-start.19) | collective-permute-done | bytes 2097184 | tf_op jit(solution)/shard_map/ppermute | solution.py:34
  424.2 2.2 collective-permute-done.20
  427.1 2.4 collective-permute-start.22
  429.4 2.0 collective-permute-start.21
  432.9 1.7 broadcast_select_fusion
  436.4 2.8 collective-permute-done.22
  439.9 5.1 %concatenate.56 = bf16[340,1024]{1,0:T(8,128)(2,1)} concatenate(bf16[60,1024]{1,0:T(8,128)(2,1)S(1)} %get-tuple-element.277, bf16[60,1024]{1,0:T(8,128)(2,1)} %copy-done.35, bf16[60,1024]{1,0:T(8,128)(2,1)S(1)} %collective-permute-done.22, bf16[60,1024]{1,0:T(8,128)(2,1)S(1)} %collective-permute-done.23, bf16[100,1024]{1,0:T(8,128)(2,1)S(1)} %convolution_convert_fusion.12), dimensions={0} | concatenate | bytes 1392640 | tf_op jit(solution)/shard_map/concatenate | solution.py:244
  445.1 1.7 collective-permute-done.25
  446.7 1.7 collective-permute-done.24
  448.5 2.5 fusion.23
  452.8 2.0 convert_add_fusion
  454.8 1.7 convert_add_fusion.2
  458.7 2.5 maximum_bitcast_fusion
  462.8 21.0 %collective-permute-done.29 = bf16[160,1024]{1,0:T(8,128)(2,1)S(1)} collective-permute-done((bf16[160,1024]{1,0:T(8,128)(2,1)S(1)}, bf16[160,1024]{1,0:T(8,128)(2,1)S(1)}, u32[]{:S(2)}, u32[]{:S(2)}) %collective-permute-start.29) | collective-permute-done | bytes 327712 | tf_op jit(solution)/shard_map/ppermute | solution.py:34
  488.1 2.5 pad_maximum_fusion
  490.6 2.7 collective-permute-done.30
  493.4 3.9 collective-permute-done.28
  499.5 1.6 copy.90
  (286 shorter events, 58.1 us)
Async XLA Ops:
  7.2 8.8 %copy-start = (bf16[100,1024]{1,0:T(8,128)(2,1)S(1)}, bf16[100,1024]{1,0:T(8,128)(2,1)}, u32[]{:S(2)}) copy-start(bf16[100,1024]{1,0:T(8,128)(2,1)} %param.11) | copy-start | bytes 614404
  7.2 8.8 %copy-start.40 = (s32[384]{0:T(512)S(1)}, s32[384]{0:T(512)}, u32[]{:S(2)}) copy-start(s32[384]{0:T(512)} %param.9) | copy-start | bytes 4612
  7.2 8.8 %copy-start.36 = (s32[384]{0:T(512)S(1)}, s32[384]{0:T(512)}, u32[]{:S(2)}) copy-start(s32[384]{0:T(512)} %param.10) | copy-start | bytes 4612
  7.2 8.8 %copy-start.30 = (bf16[384,1024]{1,0:T(8,128)(2,1)S(1)}, bf16[384,1024]{1,0:T(8,128)(2,1)}, u32[]{:S(2)}) copy-start(bf16[384,1024]{1,0:T(8,128)(2,1)} %param.8) | copy-start | bytes 2359300
  7.2 87.7 %all-gather.3.cloned.1.call-start = ((), (), s32[]{:S(2)}) async-start(), calls=%async_computation.2 | async-start | bytes 3932160 | tf_op jit(solution)/shard_map/all_gather | solution.py:151
  9.7 149.4 %all-gather.5.cloned.1.call-start = ((), (), s32[]{:S(2)}) async-start(), calls=%async_computation.3 | async-start | bytes 3932160 | tf_op jit(solution)/shard_map/all_gather | solution.py:152
  9.9 23.7 %copy-start.33 = (bf16[1024,60]{0,1:T(8,128)(2,1)}, bf16[1024,60]{0,1:T(8,128)(2,1)S(1)}, u32[]{:S(2)}) copy-start(bf16[1024,60]{0,1:T(8,128)(2,1)S(1)} %get-tuple-element.270) | copy-start | bytes 368644
  9.9 9.4 %collective-permute-start = (bf16[1024,60]{0,1:T(8,128)(2,1)S(1)}, bf16[1024,60]{0,1:T(8,128)(2,1)S(1)}, u32[]{:S(2)}, u32[]{:S(2)}) collective-permute-start(bf16[1024,60]{0,1:T(8,128)(2,1)S(1)} %get-tuple-element.271), channel_id=1, source_target_pairs={{0,1},{1,2},{2,3},{3,0},{4,5},{5,6},{6,7},{7,4},{8,9},{9,10},{10,1... | collective-permute-start | bytes 368648 | tf_op jit(solution)/shard_map/ppermute | solution.py:29
  12.9 7.8 %collective-permute-start.2 = (bf16[1024,60]{0,1:T(8,128)(2,1)S(1)}, bf16[1024,60]{0,1:T(8,128)(2,1)S(1)}, u32[]{:S(2)}, u32[]{:S(2)}) collective-permute-start(bf16[1024,60]{0,1:T(8,128)(2,1)S(1)} %get-tuple-element.272), channel_id=1, source_target_pairs={{0,3},{1,0},{2,1},{3,2},{4,7},{5,4},{6,5},{7,6},{8,11},{9,8},{10,9... | collective-permute-start | bytes 368648 | tf_op jit(solution)/shard_map/ppermute | solution.py:29
  15.0 18.1 %collective-permute-start.1 = (bf16[1024,60]{0,1:T(8,128)(2,1)S(1)}, bf16[1024,60]{0,1:T(8,128)(2,1)S(1)}, u32[]{:S(2)}, u32[]{:S(2)}) collective-permute-start(bf16[1024,60]{0,1:T(8,128)(2,1)S(1)} %get-tuple-element.273), channel_id=1, source_target_pairs={{0,2},{1,3},{2,0},{3,1},{4,6},{5,7},{6,4},{7,5},{8,10},{9,11},{10,... | collective-permute-start | bytes 368648 | tf_op jit(solution)/shard_map/ppermute | solution.py:29
  16.0 17.6 %copy-start.38 = (pred[384]{0:T(512)(128)(4,1)}, pred[384]{0:T(512)(128)(4,1)S(1)}, u32[]{:S(2)}) copy-start(pred[384]{0:T(512)(128)(4,1)S(1)} %broadcast_compare_fusion) | copy-start | bytes 1156
  16.4 68.5 %copy-start.3 = (bf16[384,1024]{1,0:T(8,128)(2,1)}, bf16[384,1024]{1,0:T(8,128)(2,1)S(1)}, u32[]{:S(2)}) copy-start(bf16[384,1024]{1,0:T(8,128)(2,1)S(1)} %fusion.25) | copy-start | bytes 2359300
  16.5 23.2 %collective-permute-start.6 = (bf16[7,1024]{1,0:T(8,128)(2,1)S(1)}, bf16[7,1024]{1,0:T(8,128)(2,1)S(1)}, u32[]{:S(2)}, u32[]{:S(2)}) collective-permute-start(bf16[7,1024]{1,0:T(8,128)(2,1)S(1)} %get-tuple-element.268), channel_id=1, source_target_pairs={{0,4},{4,8},{8,12},{12,16},{16,20},{20,24},{24,28},{1,5},{5,9},{9,... | collective-permute-start | bytes 43016 | tf_op jit(solution)/shard_map/ppermute | solution.py:14
  17.8 21.9 %collective-permute-start.7 = (bf16[7,1024]{1,0:T(8,128)(2,1)S(1)}, bf16[7,1024]{1,0:T(8,128)(2,1)S(1)}, u32[]{:S(2)}, u32[]{:S(2)}) collective-permute-start(bf16[7,1024]{1,0:T(8,128)(2,1)S(1)} %get-tuple-element.269), channel_id=1, source_target_pairs={{4,0},{8,4},{12,8},{16,12},{20,16},{24,20},{28,24},{5,1},{9,5},{13... | collective-permute-start | bytes 43016 | tf_op jit(solution)/shard_map/ppermute | solution.py:15
  19.3 20.6 %copy-start.41 = (bf16[1024,60]{0,1:T(8,128)(2,1)}, bf16[1024,60]{0,1:T(8,128)(2,1)S(1)}, u32[]{:S(2)}) copy-start(bf16[1024,60]{0,1:T(8,128)(2,1)S(1)} %collective-permute-done) | copy-start | bytes 368644
  20.7 19.2 %copy-start.43 = (bf16[1024,60]{0,1:T(8,128)(2,1)}, bf16[1024,60]{0,1:T(8,128)(2,1)S(1)}, u32[]{:S(2)}) copy-start(bf16[1024,60]{0,1:T(8,128)(2,1)S(1)} %collective-permute-done.2) | copy-start | bytes 368644
  33.1 6.8 %copy-start.45 = (bf16[1024,60]{0,1:T(8,128)(2,1)}, bf16[1024,60]{0,1:T(8,128)(2,1)S(1)}, u32[]{:S(2)}) copy-start(bf16[1024,60]{0,1:T(8,128)(2,1)S(1)} %collective-permute-done.1) | copy-start | bytes 368644
  33.8 15.9 %collective-permute-start.3 = (f32[384,60]{1,0:T(8,128)S(1)}, f32[384,60]{1,0:T(8,128)S(1)}, u32[]{:S(2)}, u32[]{:S(2)}) collective-permute-start(f32[384,60]{1,0:T(8,128)S(1)} %get-tuple-element.278), channel_id=1, source_target_pairs={{0,3},{1,0},{2,1},{3,2},{4,7},{5,4},{6,5},{7,6},{8,11},{9,8},{10,9... | collective-permute-start | bytes 276488 | tf_op jit(solution)/shard_map/ppermute | solution.py:29
  39.0 36.7 %collective-permute-start.4 = (f32[384,60]{1,0:T(8,128)S(1)}, f32[384,60]{1,0:T(8,128)S(1)}, u32[]{:S(2)}, u32[]{:S(2)}) collective-permute-start(f32[384,60]{1,0:T(8,128)S(1)} %get-tuple-element.279), channel_id=1, source_target_pairs={{0,2},{1,3},{2,0},{3,1},{4,6},{5,7},{6,4},{7,5},{8,10},{9,11},{10,... | collective-permute-start | bytes 276488 | tf_op jit(solution)/shard_map/ppermute | solution.py:29
  39.0 36.7 %collective-permute-start.5 = (f32[384,60]{1,0:T(8,128)S(1)}, f32[384,60]{1,0:T(8,128)S(1)}, u32[]{:S(2)}, u32[]{:S(2)}) collective-permute-start(f32[384,60]{1,0:T(8,128)S(1)} %get-tuple-element.280), channel_id=1, source_target_pairs={{0,1},{1,2},{2,3},{3,0},{4,5},{5,6},{6,7},{7,4},{8,9},{9,10},{10,1... | collective-permute-start | bytes 276488 | tf_op jit(solution)/shard_map/ppermute | solution.py:29
  39.9 44.6 %copy-start.28 = (bf16[398,1024]{1,0:T(8,128)(2,1)}, bf16[398,1024]{1,0:T(8,128)(2,1)S(1)}, u32[]{:S(2)}) copy-start(bf16[398,1024]{1,0:T(8,128)(2,1)S(1)} %pad_maximum_fusion.1) | copy-start | bytes 2445316
  86.1 238.3 %reduce-scatter.5.cloned.1.call-start = ((), (), s32[]{:S(2)}) async-start(), calls=%async_computation.5 | async-start | bytes 3932160 | tf_op jit(solution)/shard_map/reduce_scatter | solution.py:161
  175.7 12.0 %copy-start.67 = (bf16[384,2048]{1,0:T(8,128)(2,1)}, bf16[384,2048]{1,0:T(8,128)(2,1)S(1)}, u32[]{:S(2)}) copy-start(bf16[384,2048]{1,0:T(8,128)(2,1)S(1)} %get-tuple-element.39) | copy-start | bytes 4718596
  187.7 260.8 %reduce-scatter.3.cloned.1.call-start = ((), (), s32[]{:S(2)}) async-start(), calls=%async_computation.4 | async-start | bytes 3932160 | tf_op jit(solution)/shard_map/reduce_scatter | solution.py:171
  238.4 61.0 %collective-permute-start.8 = (bf16[2,2,512,1024]{2,3,1,0:T(8,128)(2,1)}, bf16[2,2,512,1024]{2,3,1,0:T(8,128)(2,1)}, u32[]{:S(2)}, u32[]{:S(2)}) collective-permute-start(bf16[2,2,512,1024]{2,3,1,0:T(8,128)(2,1)} %copy.67), channel_id=1, source_target_pairs={{0,4},{4,0},{8,12},{12,8},{16,20},{20,16},{24,28},{28,24},{1,5},{5... | collective-permute-start | bytes 12582920 | tf_op jit(solution)/shard_map/ppermute | solution.py:34
  239.6 66.8 %collective-permute-start.10 = (bf16[2,2,512,1024]{3,2,1,0:T(8,128)(2,1)}, bf16[2,2,512,1024]{3,2,1,0:T(8,128)(2,1)}, u32[]{:S(2)}, u32[]{:S(2)}) collective-permute-start(bf16[2,2,512,1024]{3,2,1,0:T(8,128)(2,1)} %bitcast.138), channel_id=1, source_target_pairs={{0,4},{4,0},{8,12},{12,8},{16,20},{20,16},{24,28},{28,24},{1,5},{5... | collective-permute-start | bytes 12582920 | tf_op jit(solution)/shard_map/ppermute | solution.py:34
  246.9 65.4 %collective-permute-start.9 = (bf16[2,2,512,1024]{2,3,1,0:T(8,128)(2,1)}, bf16[2,2,512,1024]{2,3,1,0:T(8,128)(2,1)}, u32[]{:S(2)}, u32[]{:S(2)}) collective-permute-start(bf16[2,2,512,1024]{2,3,1,0:T(8,128)(2,1)} %copy.69), channel_id=1, source_target_pairs={{0,4},{4,0},{8,12},{12,8},{16,20},{20,16},{24,28},{28,24},{1,5},{5... | collective-permute-start | bytes 12582920 | tf_op jit(solution)/shard_map/ppermute | solution.py:34
  248.0 69.9 %collective-permute-start.11 = (bf16[2,2,512,1024]{3,2,1,0:T(8,128)(2,1)}, bf16[2,2,512,1024]{3,2,1,0:T(8,128)(2,1)}, u32[]{:S(2)}, u32[]{:S(2)}) collective-permute-start(bf16[2,2,512,1024]{3,2,1,0:T(8,128)(2,1)} %bitcast.137), channel_id=1, source_target_pairs={{0,4},{4,0},{8,12},{12,8},{16,20},{20,16},{24,28},{28,24},{1,5},{5... | collective-permute-start | bytes 12582920 | tf_op jit(solution)/shard_map/ppermute | solution.py:34
  281.3 6.3 %copy-start.66 = (bf16[384,2048]{1,0:T(8,128)(2,1)S(1)}, bf16[384,2048]{1,0:T(8,128)(2,1)}, u32[]{:S(2)}) copy-start(bf16[384,2048]{1,0:T(8,128)(2,1)} %get-tuple-element.40) | copy-start | bytes 4718596
  299.4 7.0 %copy-start.13 = (bf16[2048,1024]{1,0:T(8,128)(2,1)S(1)}, bf16[2048,1024]{1,0:T(8,128)(2,1)}, u32[]{:S(2)}) copy-start(bf16[2048,1024]{1,0:T(8,128)(2,1)} %convolution_convert_fusion.3) | copy-start | bytes 12582916
  317.9 6.5 %copy-start.14 = (bf16[384,1024]{1,0:T(8,128)(2,1)S(1)}, bf16[384,1024]{1,0:T(8,128)(2,1)}, u32[]{:S(2)}) copy-start(bf16[384,1024]{1,0:T(8,128)(2,1)} %param.15) | copy-start | bytes 2359300
  324.4 9.3 %copy-start.17 = (bf16[2,512,1024]{2,1,0:T(8,128)(2,1)S(1)}, bf16[2,512,1024]{2,1,0:T(8,128)(2,1)}, u32[]{:S(2)}) copy-start(bf16[2,512,1024]{2,1,0:T(8,128)(2,1)} %get-tuple-element.54) | copy-start | bytes 6291460
  326.0 18.4 %collective-permute-start.13 = (bf16[7,1084]{1,0:T(8,128)(2,1)S(1)}, bf16[7,1084]{1,0:T(8,128)(2,1)S(1)}, u32[]{:S(2)}, u32[]{:S(2)}) collective-permute-start(bf16[7,1084]{1,0:T(8,128)(2,1)S(1)} %pad_maximum_fusion.11), channel_id=1, source_target_pairs={{4,0},{8,4},{12,8},{16,12},{20,16},{24,20},{28,24},{5,1},{9,5},{13... | collective-permute-start | bytes 45536 | tf_op jit(solution)/shard_map/ppermute | solution.py:15
  327.3 8.4 %copy-start.29 = (bf16[398,1024]{1,0:T(8,128)(2,1)S(1)}, bf16[398,1024]{1,0:T(8,128)(2,1)}, u32[]{:S(2)}) copy-start(bf16[398,1024]{1,0:T(8,128)(2,1)} %copy-done.28) | copy-start | bytes 2445316
  327.4 17.8 %collective-permute-start.12 = (bf16[7,1084]{1,0:T(8,128)(2,1)S(1)}, bf16[7,1084]{1,0:T(8,128)(2,1)S(1)}, u32[]{:S(2)}, u32[]{:S(2)}) collective-permute-start(bf16[7,1084]{1,0:T(8,128)(2,1)S(1)} %pad_maximum_fusion.10), channel_id=1, source_target_pairs={{0,4},{4,8},{8,12},{12,16},{16,20},{20,24},{24,28},{1,5},{5,9},{9,... | collective-permute-start | bytes 45536 | tf_op jit(solution)/shard_map/ppermute | solution.py:14
  330.7 48.5 %collective-permute-start.14 = (bf16[2,512,1024]{1,2,0:T(8,128)(2,1)}, bf16[2,512,1024]{1,2,0:T(8,128)(2,1)S(1)}, u32[]{:S(2)}, u32[]{:S(2)}) collective-permute-start(bf16[2,512,1024]{1,2,0:T(8,128)(2,1)} %get-tuple-element.51), channel_id=1, source_target_pairs={{0,16},{4,20},{8,24},{12,28},{16,0},{20,4},{24,8},{28,12},{1,17},{... | collective-permute-start | bytes 6291464 | tf_op jit(solution)/shard_map/ppermute | solution.py:34
  332.8 48.6 %collective-permute-start.15 = (bf16[2,512,1024]{1,2,0:T(8,128)(2,1)}, bf16[2,512,1024]{1,2,0:T(8,128)(2,1)S(1)}, u32[]{:S(2)}, u32[]{:S(2)}) collective-permute-start(bf16[2,512,1024]{1,2,0:T(8,128)(2,1)} %get-tuple-element.52), channel_id=1, source_target_pairs={{0,8},{4,12},{8,0},{12,4},{16,24},{20,28},{24,16},{28,20},{1,9},{5... | collective-permute-start | bytes 6291464 | tf_op jit(solution)/shard_map/ppermute | solution.py:34
  333.7 90.5 %collective-permute-start.19 = (bf16[2,512,1024]{2,1,0:T(8,128)(2,1)S(1)}, bf16[2,512,1024]{2,1,0:T(8,128)(2,1)S(1)}, u32[]{:S(2)}, u32[]{:S(2)}) collective-permute-start(bf16[2,512,1024]{2,1,0:T(8,128)(2,1)S(1)} %copy-done.17), channel_id=1, source_target_pairs={{0,16},{4,20},{8,24},{12,28},{16,0},{20,4},{24,8},{28,12},{1,17},{... | collective-permute-start | bytes 6291464 | tf_op jit(solution)/shard_map/ppermute | solution.py:34
  337.8 6.6 %copy-start.18 = (bf16[2,512,1024]{2,1,0:T(8,128)(2,1)S(1)}, bf16[2,512,1024]{2,1,0:T(8,128)(2,1)}, u32[]{:S(2)}) copy-start(bf16[2,512,1024]{2,1,0:T(8,128)(2,1)} %get-tuple-element.55) | copy-start | bytes 6291460
  344.4 81.9 %collective-permute-start.20 = (bf16[2,512,1024]{2,1,0:T(8,128)(2,1)S(1)}, bf16[2,512,1024]{2,1,0:T(8,128)(2,1)S(1)}, u32[]{:S(2)}, u32[]{:S(2)}) collective-permute-start(bf16[2,512,1024]{2,1,0:T(8,128)(2,1)S(1)} %copy-done.18), channel_id=1, source_target_pairs={{0,8},{4,12},{8,0},{12,4},{16,24},{20,28},{24,16},{28,20},{1,9},{5... | collective-permute-start | bytes 6291464 | tf_op jit(solution)/shard_map/ppermute | solution.py:34
  353.9 30.8 %copy-start.7 = (bf16[1,2,512,1024]{2,3,1,0:T(8,128)(2,1)S(1)}, bf16[1,2,512,1024]{2,3,1,0:T(8,128)(2,1)}, u32[]{:S(2)}) copy-start(bf16[1,2,512,1024]{2,3,1,0:T(8,128)(2,1)} %get-tuple-element.254) | copy-start | bytes 6291460
  355.3 30.7 %copy-start.9 = (bf16[2,1,512,1024]{2,3,1,0:T(8,128)(2,1)S(1)}, bf16[2,1,512,1024]{2,3,1,0:T(8,128)(2,1)}, u32[]{:S(2)}) copy-start(bf16[2,1,512,1024]{2,3,1,0:T(8,128)(2,1)} %get-tuple-element.252) | copy-start | bytes 6291460
  379.2 8.0 %copy-start.21 = (bf16[2,512,1024]{1,2,0:T(8,128)(2,1)}, bf16[2,512,1024]{1,2,0:T(8,128)(2,1)S(1)}, u32[]{:S(2)}) copy-start(bf16[2,512,1024]{1,2,0:T(8,128)(2,1)S(1)} %collective-permute-done.14) | copy-start | bytes 6291460
  381.4 5.9 %collective-permute-start.18 = (bf16[384,60]{1,0:T(8,128)(2,1)S(1)}, bf16[384,60]{1,0:T(8,128)(2,1)S(1)}, u32[]{:S(2)}, u32[]{:S(2)}) collective-permute-start(bf16[384,60]{1,0:T(8,128)(2,1)S(1)} %fusion.27), channel_id=1, source_target_pairs={{0,3},{1,0},{2,1},{3,2},{4,7},{5,4},{6,5},{7,6},{8,11},{9,8},{10,9... | collective-permute-start | bytes 138248 | tf_op jit(solution)/shard_map/ppermute | solution.py:29
  383.3 8.6 %collective-permute-start.17 = (bf16[384,60]{1,0:T(8,128)(2,1)S(1)}, bf16[384,60]{1,0:T(8,128)(2,1)S(1)}, u32[]{:S(2)}, u32[]{:S(2)}) collective-permute-start(bf16[384,60]{1,0:T(8,128)(2,1)S(1)} %fusion.27), channel_id=1, source_target_pairs={{0,2},{1,3},{2,0},{3,1},{4,6},{5,7},{6,4},{7,5},{8,10},{9,11},{10,... | collective-permute-start | bytes 138248 | tf_op jit(solution)/shard_map/ppermute | solution.py:29
  383.3 10.1 %collective-permute-start.16 = (bf16[384,60]{1,0:T(8,128)(2,1)S(1)}, bf16[384,60]{1,0:T(8,128)(2,1)S(1)}, u32[]{:S(2)}, u32[]{:S(2)}) collective-permute-start(bf16[384,60]{1,0:T(8,128)(2,1)S(1)} %fusion.27), channel_id=1, source_target_pairs={{0,1},{1,2},{2,3},{3,0},{4,5},{5,6},{6,7},{7,4},{8,9},{9,10},{10,1... | collective-permute-start | bytes 138248 | tf_op jit(solution)/shard_map/ppermute | solution.py:29
  386.0 40.4 %copy-start.4 = (bf16[384,1024]{1,0:T(8,128)(2,1)S(1)}, bf16[384,1024]{1,0:T(8,128)(2,1)}, u32[]{:S(2)}) copy-start(bf16[384,1024]{1,0:T(8,128)(2,1)} %copy-done.3) | copy-start | bytes 2359300
  387.3 59.4 %collective-permute-start.25 = (bf16[512,1024]{0,1:T(8,128)(2,1)}, bf16[512,1024]{0,1:T(8,128)(2,1)}, u32[]{:S(2)}, u32[]{:S(2)}) collective-permute-start(bf16[512,1024]{0,1:T(8,128)(2,1)} %fusion.31), channel_id=1, source_target_pairs={{0,16},{4,20},{8,24},{12,28},{16,0},{20,4},{24,8},{28,12},{1,17},{... | collective-permute-start | bytes 3145736 | tf_op jit(solution)/shard_map/ppermute | solution.py:34
  391.9 56.6 %collective-permute-start.24 = (bf16[512,1024]{0,1:T(8,128)(2,1)}, bf16[512,1024]{0,1:T(8,128)(2,1)}, u32[]{:S(2)}, u32[]{:S(2)}) collective-permute-start(bf16[512,1024]{0,1:T(8,128)(2,1)} %fusion.30), channel_id=1, source_target_pairs={{0,8},{4,12},{8,0},{12,4},{16,24},{20,28},{24,16},{28,20},{1,9},{5... | collective-permute-start | bytes 3145736 | tf_op jit(solution)/shard_map/ppermute | solution.py:34
  424.1 8.7 %copy-start.19 = (bf16[2,512,1024]{2,1,0:T(8,128)(2,1)}, bf16[2,512,1024]{2,1,0:T(8,128)(2,1)S(1)}, u32[]{:S(2)}) copy-start(bf16[2,512,1024]{2,1,0:T(8,128)(2,1)S(1)} %collective-permute-done.19) | copy-start | bytes 6291460
  426.4 8.6 %copy-start.24 = (bf16[2,512,1024]{2,1,0:T(8,128)(2,1)}, bf16[2,512,1024]{2,1,0:T(8,128)(2,1)S(1)}, u32[]{:S(2)}) copy-start(bf16[2,512,1024]{2,1,0:T(8,128)(2,1)S(1)} %collective-permute-done.20) | copy-start | bytes 6291460
  426.8 6.0 %copy-start.31 = (bf16[1024,384]{0,1:T(8,128)(2,1)S(1)}, bf16[1024,384]{0,1:T(8,128)(2,1)}, u32[]{:S(2)}) copy-start(bf16[1024,384]{0,1:T(8,128)(2,1)} %reduce-scatter.5.cloned.1.call-done) | copy-start | bytes 2359300
  426.9 9.5 %collective-permute-start.23 = (bf16[60,1024]{1,0:T(8,128)(2,1)S(1)}, bf16[60,1024]{1,0:T(8,128)(2,1)S(1)}, u32[]{:S(2)}, u32[]{:S(2)}) collective-permute-start(bf16[60,1024]{1,0:T(8,128)(2,1)S(1)} %get-tuple-element.274), channel_id=1, source_target_pairs={{0,1},{1,2},{2,3},{3,0},{4,5},{5,6},{6,7},{7,4},{8,9},{9,10},{10,1... | collective-permute-start | bytes 368648 | tf_op jit(solution)/shard_map/ppermute | solution.py:29
  427.1 12.2 %collective-permute-start.22 = (bf16[60,1024]{1,0:T(8,128)(2,1)S(1)}, bf16[60,1024]{1,0:T(8,128)(2,1)S(1)}, u32[]{:S(2)}, u32[]{:S(2)}) collective-permute-start(bf16[60,1024]{1,0:T(8,128)(2,1)S(1)} %get-tuple-element.275), channel_id=1, source_target_pairs={{0,2},{1,3},{2,0},{3,1},{4,6},{5,7},{6,4},{7,5},{8,10},{9,11},{10,... | collective-permute-start | bytes 368648 | tf_op jit(solution)/shard_map/ppermute | solution.py:29
  429.4 9.8 %collective-permute-start.21 = (bf16[60,1024]{1,0:T(8,128)(2,1)S(1)}, bf16[60,1024]{1,0:T(8,128)(2,1)S(1)}, u32[]{:S(2)}, u32[]{:S(2)}) collective-permute-start(bf16[60,1024]{1,0:T(8,128)(2,1)S(1)} %get-tuple-element.276), channel_id=1, source_target_pairs={{0,3},{1,0},{2,1},{3,2},{4,7},{5,4},{6,5},{7,6},{8,11},{9,8},{10,9... | collective-permute-start | bytes 368648 | tf_op jit(solution)/shard_map/ppermute | solution.py:29
  435.0 13.4 %copy-start.11 = (bf16[384,1024]{1,0:T(8,128)(2,1)S(1)}, bf16[384,1024]{1,0:T(8,128)(2,1)}, u32[]{:S(2)}) copy-start(bf16[384,1024]{1,0:T(8,128)(2,1)} %fusion.21) | copy-start | bytes 2359300
  448.5 8.0 %collective-permute-start.26 = (bf16[340,1024]{1,0:T(8,128)(2,1)}, bf16[340,1024]{1,0:T(8,128)(2,1)}, u32[]{:S(2)}, u32[]{:S(2)}) collective-permute-start(bf16[340,1024]{1,0:T(8,128)(2,1)} %concatenate.56), channel_id=1, source_target_pairs={{0,4},{4,0},{8,12},{12,8},{16,20},{20,16},{24,28},{28,24},{1,5},{5... | collective-permute-start | bytes 2088968 | tf_op jit(solution)/shard_map/ppermute | solution.py:34
  451.0 33.5 %collective-permute-start.31 = (bf16[512,1024]{1,0:T(8,128)(2,1)}, bf16[512,1024]{1,0:T(8,128)(2,1)S(1)}, u32[]{:S(2)}, u32[]{:S(2)}) collective-permute-start(bf16[512,1024]{1,0:T(8,128)(2,1)} %fusion.28), channel_id=1, source_target_pairs={{0,8},{4,12},{8,0},{12,4},{16,24},{20,28},{24,16},{28,20},{1,9},{5... | collective-permute-start | bytes 3145736 | tf_op jit(solution)/shard_map/ppermute | solution.py:34
  452.2 32.9 %collective-permute-start.32 = (bf16[512,1024]{1,0:T(8,128)(2,1)}, bf16[512,1024]{1,0:T(8,128)(2,1)S(1)}, u32[]{:S(2)}, u32[]{:S(2)}) collective-permute-start(bf16[512,1024]{1,0:T(8,128)(2,1)} %fusion.29), channel_id=1, source_target_pairs={{0,16},{4,20},{8,24},{12,28},{16,0},{20,4},{24,8},{28,12},{1,17},{... | collective-permute-start | bytes 3145736 | tf_op jit(solution)/shard_map/ppermute | solution.py:34
  457.9 25.9 %collective-permute-start.29 = (bf16[160,1024]{1,0:T(8,128)(2,1)S(1)}, bf16[160,1024]{1,0:T(8,128)(2,1)S(1)}, u32[]{:S(2)}, u32[]{:S(2)}) collective-permute-start(bf16[160,1024]{1,0:T(8,128)(2,1)S(1)} %slice.824), channel_id=1, source_target_pairs={{0,8},{4,12},{8,0},{12,4},{16,24},{20,28},{24,16},{28,20},{1,9},{5... | collective-permute-start | bytes 983048 | tf_op jit(solution)/shard_map/ppermute | solution.py:34
  458.7 25.7 %copy-start.20 = (bf16[2,512,1024]{2,1,0:T(8,128)(2,1)S(1)}, bf16[2,512,1024]{2,1,0:T(8,128)(2,1)}, u32[]{:S(2)}) copy-start(bf16[2,512,1024]{2,1,0:T(8,128)(2,1)} %copy-done.19) | copy-start | bytes 6291460
  461.2 25.5 %collective-permute-start.27 = (bf16[180,1024]{1,0:T(8,128)(2,1)S(1)}, bf16[180,1024]{1,0:T(8,128)(2,1)S(1)}, u32[]{:S(2)}, u32[]{:S(2)}) collective-permute-start(bf16[180,1024]{1,0:T(8,128)(2,1)S(1)} %slice.822), channel_id=1, source_target_pairs={{0,16},{4,20},{8,24},{12,28},{16,0},{20,4},{24,8},{28,12},{1,17},{... | collective-permute-start | bytes 1105928 | tf_op jit(solution)/shard_map/ppermute | solution.py:34
  483.9 9.4 %collective-permute-start.30 = (bf16[160,1024]{1,0:T(8,128)(2,1)S(1)}, bf16[160,1024]{1,0:T(8,128)(2,1)S(1)}, u32[]{:S(2)}, u32[]{:S(2)}) collective-permute-start(bf16[160,1024]{1,0:T(8,128)(2,1)S(1)} %add_convert_fusion.12), channel_id=1, source_target_pairs={{0,16},{4,20},{8,24},{12,28},{16,0},{20,4},{24,8},{28,12},{1,17},{... | collective-permute-start | bytes 983048 | tf_op jit(solution)/shard_map/ppermute | solution.py:34
  486.8 10.4 %collective-permute-start.28 = (bf16[180,1024]{1,0:T(8,128)(2,1)S(1)}, bf16[180,1024]{1,0:T(8,128)(2,1)S(1)}, u32[]{:S(2)}, u32[]{:S(2)}) collective-permute-start(bf16[180,1024]{1,0:T(8,128)(2,1)S(1)} %add_convert_fusion.10), channel_id=1, source_target_pairs={{0,8},{4,12},{8,0},{12,4},{16,24},{20,28},{24,16},{28,20},{1,9},{5... | collective-permute-start | bytes 1105928 | tf_op jit(solution)/shard_map/ppermute | solution.py:34
  (43 other events, 119.2 us)
Sparse Core Ops, SparseCore 0:
  10.2 84.6 all-gather.2
  96.5 62.5 all-gather.4
  187.8 58.9 reduce-scatter.4
  299.5 59.2 reduce-scatter.2

commit v3 on v2

--- a/solution.py
+++ b/solution.py
@@ -1,6 +1,7 @@
 import jax
 import jax.numpy as jnp
 from jax import lax
+from jax.experimental.layout import Layout, with_layout_constraint
 from jax.sharding import PartitionSpec as P
 
 KW = 15
@@ -38,6 +39,10 @@
     return (lax.axis_index("seq") // (1 << bit)) % 2
 
 
+def row_major(block):
+    return with_layout_constraint(block, Layout(major_to_minor=(0, 1)))
+
+
 def seq_bits():
     return lax.axis_size("seq").bit_length() - 1
 
@@ -51,14 +56,21 @@
 
 
 def first_halves(features, factor):
-    count, depth = seq_bits(), features.shape[0]
+    count = seq_bits()
     rows = features.shape[1] >> count
-    grouped = features.reshape(depth, 1 << (count - 1), 2, rows)
     width = factor.shape[1] // 2
     shape = (2,) * (count - 1) + (rows, width)
     mine = my_bit(0)
-    other = lax.dynamic_index_in_dim(grouped, 1 - mine, 2, keepdims=False).reshape(depth, -1)
-    own = lax.dynamic_index_in_dim(grouped, mine, 2, keepdims=False).reshape(depth, -1)
+
+    def blocks(which):
+        result = []
+        for pair in range(0, 1 << count, 2):
+            low = features[:, pair * rows : (pair + 1) * rows]
+            high = features[:, (pair + 1) * rows : (pair + 2) * rows]
+            result.append(jnp.where(which == 0, low, high))
+        return jnp.concatenate(result, axis=1)
+
+    other, own = blocks(1 - mine), blocks(mine)
     sent = []
     for side in range(2):
         columns = factor[:, side * width : (side + 1) * width]
@@ -252,7 +264,7 @@
     for step in range(2, len(high_bits)):
         join_all(range(4), step, swap_all(range(4), step, send_all(range(4), step)))
     ends = [one.astype(f32) + two.astype(f32) for one, two in lines]
-    down_grad = jnp.concatenate(ends[:2], axis=1).T
+    down_grad = jnp.concatenate([row_major(end) for end in ends[:2]], axis=1).T
     up_grad = jnp.concatenate(ends[2:], axis=1)
     summed = seq_sum(sums)
     gen_total = tp_count * gen_cols

time: 517 us -> 460 us (0.89)
  local copies, waits for them, and re-layouts: 80.4 us -> 23.7 us
  other arithmetic: 59.8 us -> 82 us
  waiting for transfers between devices: 201 us -> 182 us
    optimization_barrier x4 -> x0, local copies, waits for them, and re-layouts: 24.9 us -> none  [the longest x2 12.5 us: body(): kept, middle = lax.optimization_barrier((kept, middle))]
    dynamic_slice x2 -> x0, local copies, waits for them, and re-layouts: 16 us -> none  [the longest x1 12 us: first_halves(): lax.dynamic_index_in_dim(grouped, mine, 2, keepdims=False)]
    unnamed x145 -> x191, local copies, waits for them, and re-layouts: 20.4 us -> 9.92 us
    eq x30, other arithmetic: 4.67 us -> 14.1 us  [body(): taps_at[None, :] == head * KW + tap]
    all_gather x1, waiting for transfers between devices: 6.54 us -> 0.01 us  [body(): full_cot = lax.all_gather(cotangent, 'tp', axis=1, tiled=True)]
    ppermute x17, waiting for transfers between devices: 89.9 us -> 83.4 us  [swapped(): return lax.ppermute(block, 'seq', [(i, i ^ 1 << bit) for i in range(count)])]
    reshape x1 -> x0, local copies, waits for them, and re-layouts: 6.32 us -> none  [first_halves(): grouped = features.reshape(depth, 1 << count - 1, 2, rows)]
    select_n x0 -> x2, other arithmetic: none -> 6.24 us  [blocks(): result.append(jnp.where(which == 0, low, high))]
  transfers between devices with their start and end apart: 37 -> 37, of which waited for: 18 -> 15; matrix products, arithmetic and copies ran while one was open for 42% -> 40% of each run, Pallas kernels for 0% -> 0%
where the time goes in v3:
time: 460 us; the launch traced here: 452 us
  waiting for transfers between devices  182 us (40%)
  matrix products  108 us (23%)
  other arithmetic  82 us (18%)
  starting transfers between devices  40.9 us (9%)
  local copies, waits for them, and re-layouts  23.7 us (5%)
  between operations  15.6 us (3%)
    dot_general x29, matrix products, dot(): lax.dot_general(a, b, (dims, ((), ())), preferred_element_type=jnp.float32)  100 us
    ppermute x17, waiting for transfers between devices, swapped(): return lax.ppermute(block, 'seq', [(i, i ^ 1 << bit) for i in range(count)])  83.4 us
    ppermute x12, waiting for transfers between devices, turned(): lax.ppermute(block, 'tp', [(i, (i + shift) % count) for i in range(count)])  52.9 us
    all_gather x1, waiting for transfers between devices, body(): full_act = lax.all_gather(act, 'tp', axis=1, tiled=True)  44.8 us
    convert_element_type x8, other arithmetic, chosen(): return total.astype(jnp.bfloat16)  32.3 us
    ppermute x12, starting transfers between devices, turned(): lax.ppermute(block, 'tp', [(i, (i + shift) % count) for i in range(count)])  19.6 us
    eq x30, other arithmetic, body(): taps_at[None, :] == head * KW + tap  14.1 us
    ppermute x17, starting transfers between devices, swapped(): return lax.ppermute(block, 'seq', [(i, i ^ 1 << bit) for i in range(count)])  13.1 us
  transfers between devices with their start and end apart: 37, of which 15 were waited for; matrix products, arithmetic and copies ran while one was open for 40% of the time, Pallas kernels for 0%

profile of v3, /device:TPU:0, one launch (start us, length us, event | category | flops | bytes accessed | tf_op | source)
XLA Modules:
  0.0 451.8 jit_solution(15498925890050145998)
XLA Ops:
  9.2 3.1 collective-permute-start
  12.3 2.1 collective-permute-start.2
  21.9 10.4 %collective-permute-done.1 = bf16[1024,60]{0,1:T(8,128)(2,1)S(1)} collective-permute-done((bf16[1024,60]{0,1:T(8,128)(2,1)S(1)}, bf16[1024,60]{0,1:T(8,128)(2,1)S(1)}, u32[]{:S(2)}, u32[]{:S(2)}) %collective-permute-start.1) | collective-permute-done | bytes 122912 | tf_op jit(solution)/shard_map/ppermute | solution.py:30
  33.0 5.2 %collective-permute-start.3 = (f32[384,60]{1,0:T(8,128)S(1)}, f32[384,60]{1,0:T(8,128)S(1)}, u32[]{:S(2)}, u32[]{:S(2)}) collective-permute-start(f32[384,60]{1,0:T(8,128)S(1)} %get-tuple-element.308), channel_id=1, source_target_pairs={{0,3},{1,0},{2,1},{3,2},{4,7},{5,4},{6,5},{7,6},{8,11},{9,8},{10,9... | collective-permute-start | bytes 276488 | tf_op jit(solution)/shard_map/ppermute | solution.py:30
  39.2 9.8 %collective-permute-done.3 = f32[384,60]{1,0:T(8,128)S(1)} collective-permute-done((f32[384,60]{1,0:T(8,128)S(1)}, f32[384,60]{1,0:T(8,128)S(1)}, u32[]{:S(2)}, u32[]{:S(2)}) %collective-permute-start.3) | collective-permute-done | bytes 92192 | tf_op jit(solution)/shard_map/ppermute | solution.py:30
  49.0 26.2 %collective-permute-done.4 = f32[384,60]{1,0:T(8,128)S(1)} collective-permute-done((f32[384,60]{1,0:T(8,128)S(1)}, f32[384,60]{1,0:T(8,128)S(1)}, u32[]{:S(2)}, u32[]{:S(2)}) %collective-permute-start.4) | collective-permute-done | bytes 92192 | tf_op jit(solution)/shard_map/ppermute | solution.py:30
  76.2 1.6 slice_reduce_fusion.59
  77.8 1.6 slice_reduce_fusion.14
  79.4 1.6 slice_reduce_fusion.44
  81.0 1.6 slice_reduce_fusion.29
  98.2 3.1 broadcast_select_fusion.16
  101.4 12.8 %fusion.566 = f32[384,2048]{1,0:T(8,128)} fusion(bf16[384,4096]{1,0:T(8,128)(2,1)S(1)} %copy-done.15, bf16[2048,4096]{1,0:T(8,128)(2,1)} %param.14), kind=kOutput, calls=%fused_computation.919 | convolution fusion | flops 6442450944 | bytes 23068672 | tf_op jit(solution)/shard_map/dot_general | solution.py:25
  114.2 44.8 %all-gather.5.cloned.1.call-done = bf16[384,4096]{1,0:T(8,128)(2,1)} async-done(((bf16[384,1024]{1,0:T(8,128)(2,1)}), bf16[384,4096]{1,0:T(8,128)(2,1)}) %all-gather.5.cloned.1.call-update) | async-done | bytes 3145744 | tf_op jit(solution)/shard_map/all_gather | solution.py:164
  159.0 16.6 %multiply_convert_fusion = (bf16[384,2048]{1,0:T(8,128)(2,1)}, bf16[384,2048]{1,0:T(8,128)(2,1)S(1)}) fusion(f32[384,2048]{1,0:T(8,128)} %fusion.566, bf16[384,4096]{1,0:T(8,128)(2,1)} %all-gather.5.cloned.1.call-done, bf16[4096,2048]{1,0:T(8,128)(2,1)} %param.13), kind=kOutput, calls=%fused_computation.31 | convolution fusion | flops 6459752448 | bytes 26214400 | tf_op jit(solution)/shard_map/dot_general | solution.py:25
  176.8 11.5 %fusion = bf16[4096,384]{0,1:T(8,128)(2,1)} fusion(bf16[384,2048]{1,0:T(8,128)(2,1)S(1)} %get-tuple-element.39, bf16[4096,2048]{1,0:T(8,128)(2,1)} %param.13), kind=kOutput, calls=%fused_computation.2 | convolution fusion | flops 6444023808 | bytes 21495808 | tf_op jit(solution)/shard_map/dot_general | solution.py:25
  188.8 3.1 broadcast_select_fusion.12
  191.9 4.4 convolution_convert_fusion.8
  196.3 4.3 convolution_convert_fusion.9
  200.6 4.4 convolution_convert_fusion.6
  205.0 4.3 convolution_convert_fusion.7
  210.7 6.0 %convolution_convert_fusion.2 = bf16[2048,1024]{1,0:T(8,128)(2,1)} fusion(bf16[384,2048]{1,0:T(8,128)(2,1)} %copy-done.87, bf16[384,512]{1,0:T(8,128)(2,1)} %get-tuple-element.285, bf16[384,512]{1,0:T(8,128)(2,1)} %get-tuple-element.284, bf16[384,512]{1,0:T(8,128)(2,1)} %get-tuple-element.283, bf16[384,512]{1,0:T(8,128)(2,1)S(1)} %get-tuple-element.278), kind=kOutput, calls=%fused_computation.16 | convolution fusion | flops 1619001344 | bytes 6553600 | tf_op jit(solution)/shard_map/dot_general | solution.py:25
  216.8 4.7 %convolution_convert_fusion.3 = bf16[2048,1024]{1,0:T(8,128)(2,1)} fusion(bf16[384,2048]{1,0:T(8,128)(2,1)S(1)} %copy-done.89, bf16[384,512]{1,0:T(8,128)(2,1)S(1)} %copy-done.31, bf16[384,512]{1,0:T(8,128)(2,1)S(1)} %copy-done.30, bf16[384,512]{1,0:T(8,128)(2,1)S(1)} %copy-done.29, bf16[384,512]{1,0:T(8,128)(2,1)S(1)} %get-tuple-element.278), kind=kOutput, calls=%fused_computation.17 | convolution fusion | flops 1619001344 | bytes 6553600 | tf_op jit(solution)/shard_map/dot_general | solution.py:25
  221.5 4.4 convolution_convert_fusion.4
  225.8 4.3 convolution_convert_fusion.5
  230.2 8.2 %fusion.1 = bf16[4096,384]{0,1:T(8,128)(2,1)} fusion(bf16[384,2048]{1,0:T(8,128)(2,1)S(1)} %copy-done.86, bf16[2048,4096]{1,0:T(8,128)(2,1)S(1)} %bitcast.114), kind=kOutput, calls=%fused_computation.3 | convolution fusion | flops 6444023808 | bytes 21495808 | tf_op jit(solution)/shard_map/dot_general | solution.py:25
  238.4 7.8 %add_convert_fusion.1 = (bf16[1,2,512,1024]{3,2,1,0:T(8,128)(2,1)}, bf16[2,512,1024]{2,1,0:T(8,128)(2,1)}) fusion(bf16[2,2,512,1024]{3,2,1,0:T(8,128)(2,1)} %collective-permute-done.8, s32[]{:T(128)S(6)} %select_n.1247, bf16[2,2,512,1024]{3,2,1,0:T(8,128)(2,1)} %bitcast.109, s32[]{:T(128)S(6)} %select_n.1060), kind=kLoop, calls=%fused_computation.9 | loop fusion | flops 8388608 | bytes 12582920 | tf_op jit(solution)/shard_map/convert_element_type | solution.py:55
  246.2 6.0 %add_convert_fusion.3 = (bf16[1,2,512,1024]{3,2,1,0:T(8,128)(2,1)S(1)}, bf16[2,512,1024]{2,1,0:T(8,128)(2,1)}) fusion(bf16[2,2,512,1024]{3,2,1,0:T(8,128)(2,1)} %collective-permute-done.10, s32[]{:T(128)S(6)} %select_n.1247, bf16[2,2,512,1024]{3,2,1,0:T(8,128)(2,1)S(1)} %bitcast.108, s32[]{:T(128)S(6)} %select_n.1060), kind=kLoop, calls=%fused_computation.11 | loop fusion | flops 8388608 | bytes 12582920 | tf_op jit(solution)/shard_map/convert_element_type | solution.py:55
  252.2 6.5 %add_convert_fusion = (bf16[2,1,512,1024]{3,2,1,0:T(8,128)(2,1)}, bf16[2,512,1024]{2,1,0:T(8,128)(2,1)}) fusion(bf16[2,2,512,1024]{3,2,1,0:T(8,128)(2,1)} %collective-permute-done.9, s32[]{:T(128)S(6)} %select_n.1248, bf16[2,2,512,1024]{3,2,1,0:T(8,128)(2,1)S(1)} %bitcast.107, s32[]{:T(128)S(6)} %select_n.1063), kind=kLoop, calls=%fused_computation.8 | loop fusion | flops 8388608 | bytes 12582920 | tf_op jit(solution)/shard_map/convert_element_type | solution.py:55
  258.7 6.5 %add_convert_fusion.2 = (bf16[2,1,512,1024]{3,2,1,0:T(8,128)(2,1)}, bf16[2,512,1024]{2,1,0:T(8,128)(2,1)}) fusion(bf16[2,2,512,1024]{3,2,1,0:T(8,128)(2,1)} %collective-permute-done.11, s32[]{:T(128)S(6)} %select_n.1248, bf16[2,2,512,1024]{3,2,1,0:T(8,128)(2,1)S(1)} %bitcast.106, s32[]{:T(128)S(6)} %select_n.1063), kind=kLoop, calls=%fused_computation.10 | loop fusion | flops 8388608 | bytes 12582920 | tf_op jit(solution)/shard_map/convert_element_type | solution.py:55
  265.2 1.6 fusion.24
  268.2 3.6 collective-permute-start.12
  271.7 2.2 collective-permute-start.14
  275.3 1.5 select_reduce_fusion.29
  279.3 7.6 %fusion.27 = bf16[384,60]{1,0:T(8,128)(2,1)S(1)} fusion(f32[384,60]{1,0:T(8,128)S(1)} %get-tuple-element.269, f32[384]{0:T(512)S(1)} %get-tuple-element.130, f32[384]{0:T(512)S(1)} %get-tuple-element.131, f32[384]{0:T(512)S(1)} %get-tuple-element.132, f32[384]{0:T(512)S(1)} %get-tuple-element.133, f32[384]{0:T(512)S(1)} %get-tuple-element.134, ...), kind=kOutput, calls=%fused_computation.76 | convolution fusion | flops 19449360 | bytes 234240 | tf_op jit(solution)/shard_map/dot_general | solution.py:225
  291.0 1.5 convert_reduce_fusion.59
  297.8 22.6 %collective-permute-done.14 = bf16[2,512,1024]{2,1,0:T(8,128)(2,1)S(1)} collective-permute-done((bf16[2,512,1024]{2,1,0:T(8,128)(2,1)}, bf16[2,512,1024]{2,1,0:T(8,128)(2,1)S(1)}, u32[]{:S(2)}, u32[]{:S(2)}) %collective-permute-start.14) | collective-permute-done | bytes 2097184 | tf_op jit(solution)/shard_map/ppermute | solution.py:35
  320.4 2.2 collective-permute-done.15
  323.8 2.0 collective-permute-start.16
  325.8 1.4 fusion.30
  327.3 1.4 fusion.31
  329.1 3.7 collective-permute-done.17
  334.3 31.0 %collective-permute-done.19 = bf16[2,512,1024]{2,1,0:T(8,128)(2,1)S(1)} collective-permute-done((bf16[2,512,1024]{2,1,0:T(8,128)(2,1)S(1)}, bf16[2,512,1024]{2,1,0:T(8,128)(2,1)S(1)}, u32[]{:S(2)}, u32[]{:S(2)}) %collective-permute-start.19) | collective-permute-done | bytes 2097184 | tf_op jit(solution)/shard_map/ppermute | solution.py:35
  365.3 2.2 collective-permute-done.20
  368.2 1.7 collective-permute-start.22
  369.9 2.6 collective-permute-start.21
  372.5 1.4 fusion.28
  374.0 1.7 broadcast_select_fusion
  376.1 1.4 fusion.29
  377.5 2.7 collective-permute-done.22
  380.9 5.1 %concatenate.72 = bf16[340,1024]{1,0:T(8,128)(2,1)} concatenate(bf16[60,1024]{1,0:T(8,128)(2,1)S(1)} %get-tuple-element.307, bf16[60,1024]{1,0:T(8,128)(2,1)} %copy-done.36, bf16[60,1024]{1,0:T(8,128)(2,1)S(1)} %collective-permute-done.22, bf16[60,1024]{1,0:T(8,128)(2,1)S(1)} %collective-permute-done.23, bf16[100,1024]{1,0:T(8,128)(2,1)S(1)} %convolution_convert_fusion.12), dimensions={0} | concatenate | bytes 1392640 | tf_op jit(solution)/shard_map/concatenate | solution.py:256
  386.1 1.8 collective-permute-done.25
  387.9 1.7 collective-permute-done.24
  389.6 2.5 fusion.23
  393.8 2.1 convert_add_fusion
  396.0 1.9 convert_add_fusion.2
  400.1 2.5 maximum_bitcast_fusion
  402.6 5.3 %copy.57 = f32[2048,512]{1,0:T(8,128)} copy(f32[2048,512]{0,1:T(8,128)} %maximum_bitcast_fusion) | data formatting | bytes 8388608
  408.0 1.6 collective-permute-start.27
  409.6 15.4 %collective-permute-done.29 = bf16[160,1024]{1,0:T(8,128)(2,1)} collective-permute-done((bf16[160,1024]{1,0:T(8,128)(2,1)S(1)}, bf16[160,1024]{1,0:T(8,128)(2,1)}, u32[]{:S(2)}, u32[]{:S(2)}) %collective-permute-start.29) | collective-permute-done | bytes 327712 | tf_op jit(solution)/shard_map/ppermute | solution.py:35
  426.6 2.4 convert_add_fusion.6
  429.0 1.8 convert_add_fusion.4
  432.2 2.5 pad_maximum_fusion
  435.6 5.7 %collective-permute-done.28 = bf16[180,1024]{1,0:T(8,128)(2,1)S(1)} collective-permute-done((bf16[180,1024]{1,0:T(8,128)(2,1)S(1)}, bf16[180,1024]{1,0:T(8,128)(2,1)S(1)}, u32[]{:S(2)}, u32[]{:S(2)}) %collective-permute-start.28) | collective-permute-done | bytes 368672 | tf_op jit(solution)/shard_map/ppermute | solution.py:35
  443.5 1.6 copy.68
  (328 shorter events, 59.4 us)
Async XLA Ops:
  7.2 9.3 %copy-start = (bf16[100,1024]{1,0:T(8,128)(2,1)S(1)}, bf16[100,1024]{1,0:T(8,128)(2,1)}, u32[]{:S(2)}) copy-start(bf16[100,1024]{1,0:T(8,128)(2,1)} %param.11) | copy-start | bytes 614404
  7.2 9.3 %copy-start.27 = (bf16[384,1024]{1,0:T(8,128)(2,1)S(1)}, bf16[384,1024]{1,0:T(8,128)(2,1)}, u32[]{:S(2)}) copy-start(bf16[384,1024]{1,0:T(8,128)(2,1)} %param.8) | copy-start | bytes 2359300
  7.2 91.1 %all-gather.3.cloned.1.call-start = ((), (), s32[]{:S(2)}) async-start(), calls=%async_computation.2 | async-start | bytes 3932160 | tf_op jit(solution)/shard_map/all_gather | solution.py:163
  7.9 151.1 %all-gather.5.cloned.1.call-start = ((), (), s32[]{:S(2)}) async-start(), calls=%async_computation.3 | async-start | bytes 3932160 | tf_op jit(solution)/shard_map/all_gather | solution.py:164
  9.2 23.6 %copy-start.34 = (bf16[1024,60]{0,1:T(8,128)(2,1)}, bf16[1024,60]{0,1:T(8,128)(2,1)S(1)}, u32[]{:S(2)}) copy-start(bf16[1024,60]{0,1:T(8,128)(2,1)S(1)} %get-tuple-element.300) | copy-start | bytes 368644
  9.2 12.7 %collective-permute-start = (bf16[1024,60]{0,1:T(8,128)(2,1)S(1)}, bf16[1024,60]{0,1:T(8,128)(2,1)S(1)}, u32[]{:S(2)}, u32[]{:S(2)}) collective-permute-start(bf16[1024,60]{0,1:T(8,128)(2,1)S(1)} %get-tuple-element.301), channel_id=1, source_target_pairs={{0,1},{1,2},{2,3},{3,0},{4,5},{5,6},{6,7},{7,4},{8,9},{9,10},{10,1... | collective-permute-start | bytes 368648 | tf_op jit(solution)/shard_map/ppermute | solution.py:30
  12.3 9.7 %collective-permute-start.2 = (bf16[1024,60]{0,1:T(8,128)(2,1)S(1)}, bf16[1024,60]{0,1:T(8,128)(2,1)S(1)}, u32[]{:S(2)}, u32[]{:S(2)}) collective-permute-start(bf16[1024,60]{0,1:T(8,128)(2,1)S(1)} %get-tuple-element.302), channel_id=1, source_target_pairs={{0,3},{1,0},{2,1},{3,2},{4,7},{5,4},{6,5},{7,6},{8,11},{9,8},{10,9... | collective-permute-start | bytes 368648 | tf_op jit(solution)/shard_map/ppermute | solution.py:30
  14.4 18.0 %collective-permute-start.1 = (bf16[1024,60]{0,1:T(8,128)(2,1)S(1)}, bf16[1024,60]{0,1:T(8,128)(2,1)S(1)}, u32[]{:S(2)}, u32[]{:S(2)}) collective-permute-start(bf16[1024,60]{0,1:T(8,128)(2,1)S(1)} %get-tuple-element.303), channel_id=1, source_target_pairs={{0,2},{1,3},{2,0},{3,1},{4,6},{5,7},{6,4},{7,5},{8,10},{9,11},{10,... | collective-permute-start | bytes 368648 | tf_op jit(solution)/shard_map/ppermute | solution.py:30
  17.6 66.8 %copy-start.2 = (bf16[384,1024]{1,0:T(8,128)(2,1)}, bf16[384,1024]{1,0:T(8,128)(2,1)S(1)}, u32[]{:S(2)}) copy-start(bf16[384,1024]{1,0:T(8,128)(2,1)S(1)} %fusion.25) | copy-start | bytes 2359300
  17.6 21.3 %collective-permute-start.6 = (bf16[7,1024]{1,0:T(8,128)(2,1)S(1)}, bf16[7,1024]{1,0:T(8,128)(2,1)S(1)}, u32[]{:S(2)}, u32[]{:S(2)}) collective-permute-start(bf16[7,1024]{1,0:T(8,128)(2,1)S(1)} %get-tuple-element.298), channel_id=1, source_target_pairs={{0,4},{4,8},{8,12},{12,16},{16,20},{20,24},{24,28},{1,5},{5,9},{9,... | collective-permute-start | bytes 43016 | tf_op jit(solution)/shard_map/ppermute | solution.py:15
  18.9 20.0 %collective-permute-start.7 = (bf16[7,1024]{1,0:T(8,128)(2,1)S(1)}, bf16[7,1024]{1,0:T(8,128)(2,1)S(1)}, u32[]{:S(2)}, u32[]{:S(2)}) collective-permute-start(bf16[7,1024]{1,0:T(8,128)(2,1)S(1)} %get-tuple-element.299), channel_id=1, source_target_pairs={{4,0},{8,4},{12,8},{16,12},{20,16},{24,20},{28,24},{5,1},{9,5},{13... | collective-permute-start | bytes 43016 | tf_op jit(solution)/shard_map/ppermute | solution.py:16
  21.9 17.0 %copy-start.40 = (bf16[1024,60]{0,1:T(8,128)(2,1)}, bf16[1024,60]{0,1:T(8,128)(2,1)S(1)}, u32[]{:S(2)}) copy-start(bf16[1024,60]{0,1:T(8,128)(2,1)S(1)} %collective-permute-done) | copy-start | bytes 368644
  21.9 17.0 %copy-start.42 = (bf16[1024,60]{0,1:T(8,128)(2,1)}, bf16[1024,60]{0,1:T(8,128)(2,1)S(1)}, u32[]{:S(2)}) copy-start(bf16[1024,60]{0,1:T(8,128)(2,1)S(1)} %collective-permute-done.2) | copy-start | bytes 368644
  32.4 6.5 %copy-start.44 = (bf16[1024,60]{0,1:T(8,128)(2,1)}, bf16[1024,60]{0,1:T(8,128)(2,1)S(1)}, u32[]{:S(2)}) copy-start(bf16[1024,60]{0,1:T(8,128)(2,1)S(1)} %collective-permute-done.1) | copy-start | bytes 368644
  33.0 16.0 %collective-permute-start.3 = (f32[384,60]{1,0:T(8,128)S(1)}, f32[384,60]{1,0:T(8,128)S(1)}, u32[]{:S(2)}, u32[]{:S(2)}) collective-permute-start(f32[384,60]{1,0:T(8,128)S(1)} %get-tuple-element.308), channel_id=1, source_target_pairs={{0,3},{1,0},{2,1},{3,2},{4,7},{5,4},{6,5},{7,6},{8,11},{9,8},{10,9... | collective-permute-start | bytes 276488 | tf_op jit(solution)/shard_map/ppermute | solution.py:30
  38.2 36.9 %collective-permute-start.4 = (f32[384,60]{1,0:T(8,128)S(1)}, f32[384,60]{1,0:T(8,128)S(1)}, u32[]{:S(2)}, u32[]{:S(2)}) collective-permute-start(f32[384,60]{1,0:T(8,128)S(1)} %get-tuple-element.309), channel_id=1, source_target_pairs={{0,2},{1,3},{2,0},{3,1},{4,6},{5,7},{6,4},{7,5},{8,10},{9,11},{10,... | collective-permute-start | bytes 276488 | tf_op jit(solution)/shard_map/ppermute | solution.py:30
  38.2 36.9 %collective-permute-start.5 = (f32[384,60]{1,0:T(8,128)S(1)}, f32[384,60]{1,0:T(8,128)S(1)}, u32[]{:S(2)}, u32[]{:S(2)}) collective-permute-start(f32[384,60]{1,0:T(8,128)S(1)} %get-tuple-element.310), channel_id=1, source_target_pairs={{0,1},{1,2},{2,3},{3,0},{4,5},{5,6},{6,7},{7,4},{8,9},{9,10},{10,1... | collective-permute-start | bytes 276488 | tf_op jit(solution)/shard_map/ppermute | solution.py:30
  39.1 44.8 %copy-start.25 = (bf16[398,1024]{1,0:T(8,128)(2,1)}, bf16[398,1024]{1,0:T(8,128)(2,1)S(1)}, u32[]{:S(2)}) copy-start(bf16[398,1024]{1,0:T(8,128)(2,1)S(1)} %pad_maximum_fusion.5) | copy-start | bytes 2445316
  85.6 179.6 %reduce-scatter.5.cloned.1.call-start = ((), (), s32[]{:S(2)}) async-start(), calls=%async_computation.5 | async-start | bytes 3932160 | tf_op jit(solution)/shard_map/reduce_scatter | solution.py:173
  188.3 201.3 %reduce-scatter.3.cloned.1.call-start = ((), (), s32[]{:S(2)}) async-start(), calls=%async_computation.4 | async-start | bytes 3932160 | tf_op jit(solution)/shard_map/reduce_scatter | solution.py:183
  209.3 29.0 %collective-permute-start.8 = (bf16[2,2,512,1024]{3,2,1,0:T(8,128)(2,1)}, bf16[2,2,512,1024]{3,2,1,0:T(8,128)(2,1)}, u32[]{:S(2)}, u32[]{:S(2)}) collective-permute-start(bf16[2,2,512,1024]{3,2,1,0:T(8,128)(2,1)} %bitcast.1), channel_id=1, source_target_pairs={{0,4},{4,0},{8,12},{12,8},{16,20},{20,16},{24,28},{28,24},{1,5},{5... | collective-permute-start | bytes 12582920 | tf_op jit(solution)/shard_map/ppermute | solution.py:35
  209.3 36.8 %collective-permute-start.10 = (bf16[2,2,512,1024]{3,2,1,0:T(8,128)(2,1)}, bf16[2,2,512,1024]{3,2,1,0:T(8,128)(2,1)}, u32[]{:S(2)}, u32[]{:S(2)}) collective-permute-start(bf16[2,2,512,1024]{3,2,1,0:T(8,128)(2,1)} %bitcast.3), channel_id=1, source_target_pairs={{0,4},{4,0},{8,12},{12,8},{16,20},{20,16},{24,28},{28,24},{1,5},{5... | collective-permute-start | bytes 12582920 | tf_op jit(solution)/shard_map/ppermute | solution.py:35
  209.9 42.3 %collective-permute-start.9 = (bf16[2,2,512,1024]{3,2,1,0:T(8,128)(2,1)}, bf16[2,2,512,1024]{3,2,1,0:T(8,128)(2,1)}, u32[]{:S(2)}, u32[]{:S(2)}) collective-permute-start(bf16[2,2,512,1024]{3,2,1,0:T(8,128)(2,1)} %bitcast.116), channel_id=1, source_target_pairs={{0,4},{4,0},{8,12},{12,8},{16,20},{20,16},{24,28},{28,24},{1,5},{5... | collective-permute-start | bytes 12582920 | tf_op jit(solution)/shard_map/ppermute | solution.py:35
  210.0 48.7 %collective-permute-start.11 = (bf16[2,2,512,1024]{3,2,1,0:T(8,128)(2,1)}, bf16[2,2,512,1024]{3,2,1,0:T(8,128)(2,1)}, u32[]{:S(2)}, u32[]{:S(2)}) collective-permute-start(bf16[2,2,512,1024]{3,2,1,0:T(8,128)(2,1)} %bitcast.115), channel_id=1, source_target_pairs={{0,4},{4,0},{8,12},{12,8},{16,20},{20,16},{24,28},{28,24},{1,5},{5... | collective-permute-start | bytes 12582920 | tf_op jit(solution)/shard_map/ppermute | solution.py:35
  210.7 6.1 %copy-start.29 = (bf16[384,512]{1,0:T(8,128)(2,1)S(1)}, bf16[384,512]{1,0:T(8,128)(2,1)}, u32[]{:S(2)}) copy-start(bf16[384,512]{1,0:T(8,128)(2,1)} %get-tuple-element.283) | copy-start | bytes 1179652
  210.7 6.1 %copy-start.30 = (bf16[384,512]{1,0:T(8,128)(2,1)S(1)}, bf16[384,512]{1,0:T(8,128)(2,1)}, u32[]{:S(2)}) copy-start(bf16[384,512]{1,0:T(8,128)(2,1)} %get-tuple-element.284) | copy-start | bytes 1179652
  210.7 6.1 %copy-start.31 = (bf16[384,512]{1,0:T(8,128)(2,1)S(1)}, bf16[384,512]{1,0:T(8,128)(2,1)}, u32[]{:S(2)}) copy-start(bf16[384,512]{1,0:T(8,128)(2,1)} %get-tuple-element.285) | copy-start | bytes 1179652
  221.5 8.7 %slice-start = ((s8[16777216]{0:T(1024)(128)(4,1)}), s8[4194304]{0:T(1024)(128)(4,1)S(1)}, s32[]{:S(2)}) async-start(s8[16777216]{0:T(1024)(128)(4,1)} %bitcast.113), calls=%async_computation.6 | async-start | bytes 8388608
  221.5 8.7 %slice-start.1 = ((s8[16777216]{0:T(1024)(128)(4,1)}), s8[4194304]{0:T(1024)(128)(4,1)S(1)}, s32[]{:S(2)}) async-start(s8[16777216]{0:T(1024)(128)(4,1)} %bitcast.113), calls=%async_computation.7 | async-start | bytes 8388608
  238.4 7.8 %copy-start.13 = (bf16[2048,1024]{1,0:T(8,128)(2,1)S(1)}, bf16[2048,1024]{1,0:T(8,128)(2,1)}, u32[]{:S(2)}) copy-start(bf16[2048,1024]{1,0:T(8,128)(2,1)} %convolution_convert_fusion.3) | copy-start | bytes 12582916
  252.2 6.5 %copy-start.11 = (bf16[2048,1024]{1,0:T(8,128)(2,1)S(1)}, bf16[2048,1024]{1,0:T(8,128)(2,1)}, u32[]{:S(2)}) copy-start(bf16[2048,1024]{1,0:T(8,128)(2,1)} %convolution_convert_fusion.2) | copy-start | bytes 12582916
  258.7 6.5 %copy-start.14 = (bf16[384,1024]{1,0:T(8,128)(2,1)S(1)}, bf16[384,1024]{1,0:T(8,128)(2,1)}, u32[]{:S(2)}) copy-start(bf16[384,1024]{1,0:T(8,128)(2,1)} %param.15) | copy-start | bytes 2359300
  265.2 9.5 %copy-start.17 = (bf16[2,512,1024]{2,1,0:T(8,128)(2,1)S(1)}, bf16[2,512,1024]{2,1,0:T(8,128)(2,1)}, u32[]{:S(2)}) copy-start(bf16[2,512,1024]{2,1,0:T(8,128)(2,1)} %get-tuple-element.54) | copy-start | bytes 6291460
  266.8 20.1 %collective-permute-start.13 = (bf16[7,1084]{1,0:T(8,128)(2,1)S(1)}, bf16[7,1084]{1,0:T(8,128)(2,1)S(1)}, u32[]{:S(2)}, u32[]{:S(2)}) collective-permute-start(bf16[7,1084]{1,0:T(8,128)(2,1)S(1)} %pad_maximum_fusion.23), channel_id=1, source_target_pairs={{4,0},{8,4},{12,8},{16,12},{20,16},{24,20},{28,24},{5,1},{9,5},{13... | collective-permute-start | bytes 45536 | tf_op jit(solution)/shard_map/ppermute | solution.py:16
  268.1 8.6 %copy-start.26 = (bf16[398,1024]{1,0:T(8,128)(2,1)S(1)}, bf16[398,1024]{1,0:T(8,128)(2,1)}, u32[]{:S(2)}) copy-start(bf16[398,1024]{1,0:T(8,128)(2,1)} %copy-done.25) | copy-start | bytes 2445316
  268.2 19.6 %collective-permute-start.12 = (bf16[7,1084]{1,0:T(8,128)(2,1)S(1)}, bf16[7,1084]{1,0:T(8,128)(2,1)S(1)}, u32[]{:S(2)}, u32[]{:S(2)}) collective-permute-start(bf16[7,1084]{1,0:T(8,128)(2,1)S(1)} %pad_maximum_fusion.22), channel_id=1, source_target_pairs={{0,4},{4,8},{8,12},{12,16},{16,20},{20,24},{24,28},{1,5},{5,9},{9,... | collective-permute-start | bytes 45536 | tf_op jit(solution)/shard_map/ppermute | solution.py:15
  271.7 48.6 %collective-permute-start.14 = (bf16[2,512,1024]{2,1,0:T(8,128)(2,1)}, bf16[2,512,1024]{2,1,0:T(8,128)(2,1)S(1)}, u32[]{:S(2)}, u32[]{:S(2)}) collective-permute-start(bf16[2,512,1024]{2,1,0:T(8,128)(2,1)} %get-tuple-element.51), channel_id=1, source_target_pairs={{0,16},{4,20},{8,24},{12,28},{16,0},{20,4},{24,8},{28,12},{1,17},{... | collective-permute-start | bytes 6291464 | tf_op jit(solution)/shard_map/ppermute | solution.py:35
  273.9 48.7 %collective-permute-start.15 = (bf16[2,512,1024]{2,1,0:T(8,128)(2,1)}, bf16[2,512,1024]{2,1,0:T(8,128)(2,1)S(1)}, u32[]{:S(2)}, u32[]{:S(2)}) collective-permute-start(bf16[2,512,1024]{2,1,0:T(8,128)(2,1)} %get-tuple-element.52), channel_id=1, source_target_pairs={{0,8},{4,12},{8,0},{12,4},{16,24},{20,28},{24,16},{28,20},{1,9},{5... | collective-permute-start | bytes 6291464 | tf_op jit(solution)/shard_map/ppermute | solution.py:35
  274.7 90.6 %collective-permute-start.19 = (bf16[2,512,1024]{2,1,0:T(8,128)(2,1)S(1)}, bf16[2,512,1024]{2,1,0:T(8,128)(2,1)S(1)}, u32[]{:S(2)}, u32[]{:S(2)}) collective-permute-start(bf16[2,512,1024]{2,1,0:T(8,128)(2,1)S(1)} %copy-done.17), channel_id=1, source_target_pairs={{0,16},{4,20},{8,24},{12,28},{16,0},{20,4},{24,8},{28,12},{1,17},{... | collective-permute-start | bytes 6291464 | tf_op jit(solution)/shard_map/ppermute | solution.py:35
  279.3 7.7 %copy-start.18 = (bf16[2,512,1024]{2,1,0:T(8,128)(2,1)S(1)}, bf16[2,512,1024]{2,1,0:T(8,128)(2,1)}, u32[]{:S(2)}) copy-start(bf16[2,512,1024]{2,1,0:T(8,128)(2,1)} %get-tuple-element.55) | copy-start | bytes 6291460
  286.9 80.6 %collective-permute-start.20 = (bf16[2,512,1024]{2,1,0:T(8,128)(2,1)S(1)}, bf16[2,512,1024]{2,1,0:T(8,128)(2,1)S(1)}, u32[]{:S(2)}, u32[]{:S(2)}) collective-permute-start(bf16[2,512,1024]{2,1,0:T(8,128)(2,1)S(1)} %copy-done.18), channel_id=1, source_target_pairs={{0,8},{4,12},{8,0},{12,4},{16,24},{20,28},{24,16},{28,20},{1,9},{5... | collective-permute-start | bytes 6291464 | tf_op jit(solution)/shard_map/ppermute | solution.py:35
  296.5 29.3 %copy-start.6 = (bf16[1,2,512,1024]{3,2,1,0:T(8,128)(2,1)S(1)}, bf16[1,2,512,1024]{3,2,1,0:T(8,128)(2,1)}, u32[]{:S(2)}) copy-start(bf16[1,2,512,1024]{3,2,1,0:T(8,128)(2,1)} %get-tuple-element.272) | copy-start | bytes 6291460
  297.8 29.5 %copy-start.8 = (bf16[2,1,512,1024]{3,2,1,0:T(8,128)(2,1)S(1)}, bf16[2,1,512,1024]{3,2,1,0:T(8,128)(2,1)}, u32[]{:S(2)}) copy-start(bf16[2,1,512,1024]{3,2,1,0:T(8,128)(2,1)} %get-tuple-element.270) | copy-start | bytes 6291460
  320.4 8.3 %copy-start.20 = (bf16[2,512,1024]{2,1,0:T(8,128)(2,1)}, bf16[2,512,1024]{2,1,0:T(8,128)(2,1)S(1)}, u32[]{:S(2)}) copy-start(bf16[2,512,1024]{2,1,0:T(8,128)(2,1)S(1)} %collective-permute-done.14) | copy-start | bytes 6291460
  322.6 6.1 %copy-start.22 = (bf16[2,512,1024]{2,1,0:T(8,128)(2,1)}, bf16[2,512,1024]{2,1,0:T(8,128)(2,1)S(1)}, u32[]{:S(2)}) copy-start(bf16[2,512,1024]{2,1,0:T(8,128)(2,1)S(1)} %collective-permute-done.15) | copy-start | bytes 6291460
  322.6 6.1 %collective-permute-start.18 = (bf16[384,60]{1,0:T(8,128)(2,1)S(1)}, bf16[384,60]{1,0:T(8,128)(2,1)S(1)}, u32[]{:S(2)}, u32[]{:S(2)}) collective-permute-start(bf16[384,60]{1,0:T(8,128)(2,1)S(1)} %fusion.27), channel_id=1, source_target_pairs={{0,3},{1,0},{2,1},{3,2},{4,7},{5,4},{6,5},{7,6},{8,11},{9,8},{10,9... | collective-permute-start | bytes 138248 | tf_op jit(solution)/shard_map/ppermute | solution.py:30
  323.7 9.0 %collective-permute-start.17 = (bf16[384,60]{1,0:T(8,128)(2,1)S(1)}, bf16[384,60]{1,0:T(8,128)(2,1)S(1)}, u32[]{:S(2)}, u32[]{:S(2)}) collective-permute-start(bf16[384,60]{1,0:T(8,128)(2,1)S(1)} %fusion.27), channel_id=1, source_target_pairs={{0,2},{1,3},{2,0},{3,1},{4,6},{5,7},{6,4},{7,5},{8,10},{9,11},{10,... | collective-permute-start | bytes 138248 | tf_op jit(solution)/shard_map/ppermute | solution.py:30
  323.8 10.3 %collective-permute-start.16 = (bf16[384,60]{1,0:T(8,128)(2,1)S(1)}, bf16[384,60]{1,0:T(8,128)(2,1)S(1)}, u32[]{:S(2)}, u32[]{:S(2)}) collective-permute-start(bf16[384,60]{1,0:T(8,128)(2,1)S(1)} %fusion.27), channel_id=1, source_target_pairs={{0,1},{1,2},{2,3},{3,0},{4,5},{5,6},{6,7},{7,4},{8,9},{9,10},{10,1... | collective-permute-start | bytes 138248 | tf_op jit(solution)/shard_map/ppermute | solution.py:30
  327.3 40.3 %copy-start.3 = (bf16[384,1024]{1,0:T(8,128)(2,1)S(1)}, bf16[384,1024]{1,0:T(8,128)(2,1)}, u32[]{:S(2)}) copy-start(bf16[384,1024]{1,0:T(8,128)(2,1)} %copy-done.2) | copy-start | bytes 2359300
  328.7 59.2 %collective-permute-start.25 = (bf16[512,1024]{1,0:T(8,128)(2,1)}, bf16[512,1024]{1,0:T(8,128)(2,1)}, u32[]{:S(2)}, u32[]{:S(2)}) collective-permute-start(bf16[512,1024]{1,0:T(8,128)(2,1)} %fusion.31), channel_id=1, source_target_pairs={{0,16},{4,20},{8,24},{12,28},{16,0},{20,4},{24,8},{28,12},{1,17},{... | collective-permute-start | bytes 3145736 | tf_op jit(solution)/shard_map/ppermute | solution.py:35
  332.7 56.8 %collective-permute-start.24 = (bf16[512,1024]{1,0:T(8,128)(2,1)}, bf16[512,1024]{1,0:T(8,128)(2,1)}, u32[]{:S(2)}, u32[]{:S(2)}) collective-permute-start(bf16[512,1024]{1,0:T(8,128)(2,1)} %fusion.30), channel_id=1, source_target_pairs={{0,8},{4,12},{8,0},{12,4},{16,24},{20,28},{24,16},{28,20},{1,9},{5... | collective-permute-start | bytes 3145736 | tf_op jit(solution)/shard_map/ppermute | solution.py:35
  365.3 8.6 %copy-start.19 = (bf16[2,512,1024]{2,1,0:T(8,128)(2,1)}, bf16[2,512,1024]{2,1,0:T(8,128)(2,1)S(1)}, u32[]{:S(2)}) copy-start(bf16[2,512,1024]{2,1,0:T(8,128)(2,1)S(1)} %collective-permute-done.19) | copy-start | bytes 6291460
  367.5 8.6 %copy-start.23 = (bf16[2,512,1024]{2,1,0:T(8,128)(2,1)}, bf16[2,512,1024]{2,1,0:T(8,128)(2,1)S(1)}, u32[]{:S(2)}) copy-start(bf16[2,512,1024]{2,1,0:T(8,128)(2,1)S(1)} %collective-permute-done.20) | copy-start | bytes 6291460
  368.1 9.4 %collective-permute-start.23 = (bf16[60,1024]{1,0:T(8,128)(2,1)S(1)}, bf16[60,1024]{1,0:T(8,128)(2,1)S(1)}, u32[]{:S(2)}, u32[]{:S(2)}) collective-permute-start(bf16[60,1024]{1,0:T(8,128)(2,1)S(1)} %get-tuple-element.304), channel_id=1, source_target_pairs={{0,1},{1,2},{2,3},{3,0},{4,5},{5,6},{6,7},{7,4},{8,9},{9,10},{10,1... | collective-permute-start | bytes 368648 | tf_op jit(solution)/shard_map/ppermute | solution.py:30
  368.2 12.1 %collective-permute-start.22 = (bf16[60,1024]{1,0:T(8,128)(2,1)S(1)}, bf16[60,1024]{1,0:T(8,128)(2,1)S(1)}, u32[]{:S(2)}, u32[]{:S(2)}) collective-permute-start(bf16[60,1024]{1,0:T(8,128)(2,1)S(1)} %get-tuple-element.305), channel_id=1, source_target_pairs={{0,2},{1,3},{2,0},{3,1},{4,6},{5,7},{6,4},{7,5},{8,10},{9,11},{10,... | collective-permute-start | bytes 368648 | tf_op jit(solution)/shard_map/ppermute | solution.py:30
  369.9 10.4 %collective-permute-start.21 = (bf16[60,1024]{1,0:T(8,128)(2,1)S(1)}, bf16[60,1024]{1,0:T(8,128)(2,1)S(1)}, u32[]{:S(2)}, u32[]{:S(2)}) collective-permute-start(bf16[60,1024]{1,0:T(8,128)(2,1)S(1)} %get-tuple-element.306), channel_id=1, source_target_pairs={{0,3},{1,0},{2,1},{3,2},{4,7},{5,4},{6,5},{7,6},{8,11},{9,8},{10,9... | collective-permute-start | bytes 368648 | tf_op jit(solution)/shard_map/ppermute | solution.py:30
  376.1 13.4 %copy-start.10 = (bf16[384,1024]{1,0:T(8,128)(2,1)S(1)}, bf16[384,1024]{1,0:T(8,128)(2,1)}, u32[]{:S(2)}) copy-start(bf16[384,1024]{1,0:T(8,128)(2,1)} %fusion.21) | copy-start | bytes 2359300
  389.6 8.3 %collective-permute-start.26 = (bf16[340,1024]{1,0:T(8,128)(2,1)}, bf16[340,1024]{1,0:T(8,128)(2,1)}, u32[]{:S(2)}, u32[]{:S(2)}) collective-permute-start(bf16[340,1024]{1,0:T(8,128)(2,1)} %concatenate.72), channel_id=1, source_target_pairs={{0,4},{4,0},{8,12},{12,8},{16,20},{20,16},{24,28},{28,24},{1,5},{5... | collective-permute-start | bytes 2088968 | tf_op jit(solution)/shard_map/ppermute | solution.py:35
  392.1 34.5 %collective-permute-start.31 = (bf16[512,1024]{1,0:T(8,128)(2,1)}, bf16[512,1024]{1,0:T(8,128)(2,1)}, u32[]{:S(2)}, u32[]{:S(2)}) collective-permute-start(bf16[512,1024]{1,0:T(8,128)(2,1)} %fusion.28), channel_id=1, source_target_pairs={{0,8},{4,12},{8,0},{12,4},{16,24},{20,28},{24,16},{28,20},{1,9},{5... | collective-permute-start | bytes 3145736 | tf_op jit(solution)/shard_map/ppermute | solution.py:35
  393.3 35.6 %collective-permute-start.32 = (bf16[512,1024]{1,0:T(8,128)(2,1)}, bf16[512,1024]{1,0:T(8,128)(2,1)}, u32[]{:S(2)}, u32[]{:S(2)}) collective-permute-start(bf16[512,1024]{1,0:T(8,128)(2,1)} %fusion.29), channel_id=1, source_target_pairs={{0,16},{4,20},{8,24},{12,28},{16,0},{20,4},{24,8},{28,12},{1,17},{... | collective-permute-start | bytes 3145736 | tf_op jit(solution)/shard_map/ppermute | solution.py:35
  399.3 25.7 %collective-permute-start.29 = (bf16[160,1024]{1,0:T(8,128)(2,1)S(1)}, bf16[160,1024]{1,0:T(8,128)(2,1)}, u32[]{:S(2)}, u32[]{:S(2)}) collective-permute-start(bf16[160,1024]{1,0:T(8,128)(2,1)S(1)} %slice.920), channel_id=1, source_target_pairs={{0,8},{4,12},{8,0},{12,4},{16,24},{20,28},{24,16},{28,20},{1,9},{5... | collective-permute-start | bytes 983048 | tf_op jit(solution)/shard_map/ppermute | solution.py:35
  408.0 22.8 %collective-permute-start.27 = (bf16[180,1024]{1,0:T(8,128)(2,1)S(1)}, bf16[180,1024]{1,0:T(8,128)(2,1)S(1)}, u32[]{:S(2)}, u32[]{:S(2)}) collective-permute-start(bf16[180,1024]{1,0:T(8,128)(2,1)S(1)} %slice.918), channel_id=1, source_target_pairs={{0,16},{4,20},{8,24},{12,28},{16,0},{20,4},{24,8},{28,12},{1,17},{... | collective-permute-start | bytes 1105928 | tf_op jit(solution)/shard_map/ppermute | solution.py:35
  426.1 9.4 %collective-permute-start.30 = (bf16[160,1024]{1,0:T(8,128)(2,1)S(1)}, bf16[160,1024]{1,0:T(8,128)(2,1)S(1)}, u32[]{:S(2)}, u32[]{:S(2)}) collective-permute-start(bf16[160,1024]{1,0:T(8,128)(2,1)S(1)} %add_convert_fusion.12), channel_id=1, source_target_pairs={{0,16},{4,20},{8,24},{12,28},{16,0},{20,4},{24,8},{28,12},{1,17},{... | collective-permute-start | bytes 983048 | tf_op jit(solution)/shard_map/ppermute | solution.py:35
  430.9 10.4 %collective-permute-start.28 = (bf16[180,1024]{1,0:T(8,128)(2,1)S(1)}, bf16[180,1024]{1,0:T(8,128)(2,1)S(1)}, u32[]{:S(2)}, u32[]{:S(2)}) collective-permute-start(bf16[180,1024]{1,0:T(8,128)(2,1)S(1)} %add_convert_fusion.10), channel_id=1, source_target_pairs={{0,8},{4,12},{8,0},{12,4},{16,24},{20,28},{24,16},{28,20},{1,9},{5... | collective-permute-start | bytes 1105928 | tf_op jit(solution)/shard_map/ppermute | solution.py:35
  (67 other events, 143.4 us)
Sparse Core Ops, SparseCore 0:
  9.6 84.5 all-gather.2
  96.4 62.5 all-gather.4
  188.4 58.9 reduce-scatter.4
  249.6 60.2 reduce-scatter.2
